TPU v7x, 32 devices: a whole 2x2x4 slice. The times are simulated.
32 devices in a mesh: ctx: 16 (over z, y, core), fsdp: 2 (over x).
Axes of the slice: x: 2, y: 2, z: 4, core: 2. Of those that a mesh axis runs over, the one named last changes fastest.
Arguments:
- tokens_in: bfloat16 [4, 2048, 1024], P('fsdp', 'ctx'), may hold values from -6 to 6
- gain_attn: bfloat16 [1024], P('fsdp'), may hold values from 0.5 to 1.5
- shift_attn: bfloat16 [1024], P('fsdp'), may hold values from -4 to 4
- w_heads: bfloat16 [1024, 3072], P('fsdp'), may hold values from -0.1875 to 0.1875
- bias_query: bfloat16 [1024], P('fsdp'), may hold values from -4 to 4
- bias_value: bfloat16 [1024], P('fsdp'), may hold values from -0.75 to 0.75
- w_merge: bfloat16 [1024, 1024], P('fsdp'), may hold values from -0.75 to 0.75
- bias_merge: bfloat16 [1024], P('fsdp'), may hold values from -4 to 4
- gain_mlp: bfloat16 [1024], P('fsdp'), may hold values from 0.5 to 1.5
- shift_mlp: bfloat16 [1024], P('fsdp'), may hold values from -4 to 4
- w_expand: bfloat16 [1024, 4096], P('fsdp'), may hold values from -0.1875 to 0.1875
- bias_expand: bfloat16 [4096], P('fsdp'), may hold values from -4 to 4
- w_contract: bfloat16 [4096, 1024], P('fsdp'), may hold values from -0.09375 to 0.09375
- bias_contract: bfloat16 [1024], P('fsdp'), may hold values from -4 to 4
- cotangent: bfloat16 [4, 2048, 1024], P('fsdp', 'ctx'), may hold values from -6 to 6
Outputs:
- block_out: bfloat16 [4, 2048, 1024], P('fsdp', 'ctx')
- grad_tokens: float32 [4, 2048, 1024], P('fsdp', 'ctx')
- grad_gain_attn: float32 [1024], P('fsdp')
- grad_shift_attn: float32 [1024], P('fsdp')
- grad_w_heads: float32 [1024, 3072], P('fsdp')
- grad_bias_query: float32 [1024], P('fsdp')
- grad_bias_value: float32 [1024], P('fsdp')
- grad_w_merge: float32 [1024, 1024], P('fsdp')
- grad_bias_merge: float32 [1024], P('fsdp')
- grad_gain_mlp: float32 [1024], P('fsdp')
- grad_shift_mlp: float32 [1024], P('fsdp')
- grad_w_expand: float32 [1024, 4096], P('fsdp')
- grad_bias_expand: float32 [4096], P('fsdp')
- grad_w_contract: float32 [4096, 1024], P('fsdp')
- grad_bias_contract: float32 [1024], P('fsdp')
All inputs are finite; a program needn't handle non-finite values.
Results may differ from a plain program's by a relative error of at most 0.018.
Values may be sent and summed in bfloat16 or wider, within the bound.
No kernel may reach another device: no remote copies, remote signals or barrier semaphores. Data moves between devices by JAX's collectives and lax.ppermute only.
A program may use at most 384 MiB of HBM per device.

v0:
```python
import functools
import math

import jax
import jax.numpy as jnp
from jax import lax
from jax.experimental import pallas as pl
from jax.experimental.pallas import tpu as pltpu
from jax.sharding import PartitionSpec as P

HEAD = 64
EPS = 1e-05
LOWEST = -1e30
GELU_A = math.sqrt(2.0 / math.pi)
GELU_B = 0.044715
F32 = jnp.float32
BF16 = jnp.bfloat16
VMEM_BYTES = 62 * 1024 * 1024
GAIN_ATTN, SHIFT_ATTN, BIAS_QUERY, BIAS_VALUE = 0, 1, 2, 3
BIAS_MERGE, GAIN_MLP, SHIFT_MLP, BIAS_CONTRACT = 4, 5, 6, 7
BIAS_EXPAND = 8
SUM_EXPAND = 4


def mm(left, right):
    return jnp.dot(left, right, preferred_element_type=F32)


def mm_nt(left, right):
    return lax.dot_general(left, right, (((1,), (1,)), ((), ())), preferred_element_type=F32)


def mm_tn(left, right):
    return lax.dot_general(left, right, (((0,), (0,)), ((), ())), preferred_element_type=F32)


def params(**extra):
    return pltpu.CompilerParams(vmem_limit_bytes=VMEM_BYTES, **extra)


def about(us):
    return pl.CostEstimate(flops=int(us * 1.15e9), bytes_accessed=0, transcendentals=0)


def whole(shape):
    return pl.BlockSpec(shape, lambda *_: (0,) * len(shape))


def full_row(at, mine_ref, theirs_ref, row):
    half = mine_ref.shape[1] // 2
    line, lanes = row // 2, slice(row % 2 * half, (row % 2 + 1) * half)
    mine = mine_ref[line : line + 1, lanes].astype(F32)
    theirs = theirs_ref[line : line + 1, lanes].astype(F32)
    low = jnp.where(at == 0, mine, theirs)
    high = jnp.where(at == 0, theirs, mine)
    return jnp.concatenate([low, high], axis=1)


def normalise(rows):
    mean = jnp.mean(rows, axis=-1, keepdims=True)
    centered = rows - mean
    variance = jnp.mean(centered * centered, axis=-1, keepdims=True)
    inverse = lax.rsqrt(variance + EPS)
    return centered * inverse, inverse


def normalise_back(grad, unit, inverse, gain):
    scaled = grad * gain
    mean = jnp.mean(scaled, axis=-1, keepdims=True)
    along = jnp.mean(scaled * unit, axis=-1, keepdims=True)
    return inverse * (scaled - mean - unit * along)


def piece_starts(at, core, half):
    other = (1 - at) * half
    quarter = half // 2
    return (
        (pl.multiple_of(at * half, quarter), half),
        (pl.multiple_of(other + core * quarter, quarter), quarter),
        (pl.multiple_of(other + (1 - core) * quarter, quarter), quarter),
    )


def parcel_body(place, heads_ref, contract_ref, *refs):
    vectors, first_ref, mine_ref = refs[:9], refs[9], refs[10]
    quarter, shard = heads_ref.shape[0], contract_ref.shape[0]
    first_ref[:quarter, :] = heads_ref[...]
    first_ref[quarter : quarter + shard, :] = contract_ref[...]
    mine_ref[...] = jnp.zeros_like(mine_ref)
    at = 0
    width = mine_ref.shape[1]
    for vector in vectors:
        value = vector[...].astype(F32)
        size = min(value.shape[0], width)
        for begin in range(0, value.shape[0], size):
            line, lane = at // width, at % width
            piece = value[begin : begin + size].reshape(1, size)
            mine_ref[line : line + 1, lane : lane + size] = piece.astype(BF16)
            at += size
    first_ref[quarter + shard :, :] = mine_ref[...]


def parcel(place, w_heads, w_contract, vectors, shard):
    quarter, width = w_heads.shape[0] // 2, w_contract.shape[1]
    lines = -(-sum(vector.size for vector in vectors) // (16 * width)) * 16
    shapes = [(quarter + shard + lines, width), (lines, width)]
    return pl.pallas_call(
        parcel_body,
        grid_spec=pltpu.PrefetchScalarGridSpec(
            num_scalar_prefetch=1,
            grid=(1,),
            in_specs=[
                pl.BlockSpec((quarter, width), lambda i, s: (s[1], 0)),
                pl.BlockSpec((shard, width), lambda i, s: (s[4], 0)),
            ]
            + [whole(vector.shape) for vector in vectors],
            out_specs=[whole(shape) for shape in shapes],
        ),
        out_shape=[jax.ShapeDtypeStruct(shape, BF16) for shape in shapes],
        compiler_params=params(),
        cost_estimate=about(1),
        name="parcel",
    )(place, w_heads, w_contract, *vectors)


def project(at, core, normed, bias, own, near, far, out_ref, part):
    total = bias
    for (begin, size), weight in zip(piece_starts(at, core, own.shape[0]), (own, near, far)):
        total = total + mm(normed[:, pl.ds(begin, size)], weight[...])
    turned = total.T.astype(BF16)
    for head in range(turned.shape[0] // HEAD):
        piece = turned[head * HEAD : (head + 1) * HEAD, :]
        if part is None:
            out_ref[head] = piece
        else:
            out_ref[head, part] = piece


def front_query_body(place, x_ref, mine_ref, theirs_ref, own, near, far, out_ref, h_ref, bias_ref):
    at, core = place[0], place[1]
    step = pl.program_id(0)
    wide = own.shape[1]

    @pl.when(step == 0)
    def _():
        unit, _ = normalise(x_ref[...].astype(F32))
        gain = full_row(at, mine_ref, theirs_ref, GAIN_ATTN)
        shift = full_row(at, mine_ref, theirs_ref, SHIFT_ATTN)
        h_ref[...] = (unit * gain + shift).astype(BF16)
        bias_ref[0:1, :] = full_row(at, mine_ref, theirs_ref, BIAS_QUERY)

    columns = pl.ds(pl.multiple_of(step * wide, wide), wide)
    project(at, core, h_ref, bias_ref[0:1, columns], own, near, far, out_ref, None)


def front_query(place, x, mine, theirs, own, near, far):
    rows, width = x.shape
    heads = width // HEAD
    wide = 256
    return pl.pallas_call(
        front_query_body,
        grid_spec=pltpu.PrefetchScalarGridSpec(
            num_scalar_prefetch=1,
            grid=(width // wide,),
            in_specs=[whole(x.shape), whole(mine.shape), whole(theirs.shape)]
            + [pl.BlockSpec((member.shape[0], wide), lambda i, _: (0, i)) for member in (own, near, far)],
            out_specs=[
                pl.BlockSpec((wide // HEAD, HEAD, rows), lambda i, _: (i, 0, 0)),
                whole((rows, width)),
            ],
            scratch_shapes=[pltpu.VMEM((8, width), F32)],
        ),
        out_shape=[
            jax.ShapeDtypeStruct((heads, HEAD, rows), BF16),
            jax.ShapeDtypeStruct((rows, width), BF16),
        ],
        compiler_params=params(),
        cost_estimate=about(1),
        name="front_query",
    )(place, x, mine, theirs, own, near, far)


def front_rest_body(place, h_ref, mine_ref, theirs_ref, *rest):
    weights, (out_ref, bias_ref) = rest[:6], rest[6:]
    at, core = place[0], place[1]
    step = pl.program_id(0)
    wide = weights[0].shape[1]

    @pl.when(step == 0)
    def _():
        bias_ref[0:1, :] = jnp.zeros_like(bias_ref[0:1, :])
        bias_ref[1:2, :] = full_row(at, mine_ref, theirs_ref, BIAS_VALUE)

    columns = pl.ds(pl.multiple_of(step * wide, wide), wide)
    for part in range(2):
        bias = bias_ref[part : part + 1, columns]
        project(at, core, h_ref, bias, *weights[3 * part : 3 * part + 3], out_ref, part)


def front_rest(place, normed, mine, theirs, own, near, far):
    rows, width = normed.shape
    heads = width // HEAD
    wide = 256
    steps = width // wide
    specs = []
    for part in range(2):
        for member, skip in ((own, 1), (near, 0), (far, 0)):
            first = (part + skip) * steps
            specs.append(pl.BlockSpec((member.shape[0], wide), lambda i, _, first=first: (0, first + i)))
    return pl.pallas_call(
        front_rest_body,
        grid_spec=pltpu.PrefetchScalarGridSpec(
            num_scalar_prefetch=1,
            grid=(steps,),
            in_specs=[whole(normed.shape), whole(mine.shape), whole(theirs.shape)] + specs,
            out_specs=pl.BlockSpec((wide // HEAD, 2, HEAD, rows), lambda i, _: (i, 0, 0, 0)),
            scratch_shapes=[pltpu.VMEM((8, width), F32)],
        ),
        out_shape=jax.ShapeDtypeStruct((heads, 2, HEAD, rows), BF16),
        compiler_params=params(),
        cost_estimate=about(1),
        name="front_rest",
    )(place, normed, mine, theirs, *([own, near, far] * 2))


def lay_out(source, target, per, tokens, block, turned=False, scale=None):
    for src in range(source.shape[0]):
        for pair in range(per):
            piece = source[src, :, pair * tokens : (pair + 1) * tokens]
            if scale is not None:
                piece = piece * jnp.asarray(scale, BF16)
            begin = src * tokens
            if turned:
                target[pair, begin : begin + tokens, :] = piece.astype(F32).T.astype(BF16)
            else:
                inner = begin % block
                target[pair, begin // block, :, inner : inner + tokens] = piece


def allowed_at(first_key, first_query, keys, queries):
    key_at = first_key + lax.broadcasted_iota(jnp.int32, (keys, queries), 0)
    query_at = first_query + lax.broadcasted_iota(jnp.int32, (keys, queries), 1)
    return key_at <= query_at


def attend_body(per, tokens, block, chunk, query_ref, kv_ref, out_ref, outf_ref, lse_ref, q_ref, k_ref, v_ref):
    step = pl.program_id(0)

    @pl.when(step == 0)
    def _():
        lay_out(query_ref, q_ref, per, tokens, block, scale=HEAD**-0.5)
        lay_out(kv_ref.at[:, 0], k_ref, per, tokens, chunk, turned=True)
        lay_out(kv_ref.at[:, 1], v_ref, per, tokens, chunk)

    queries = [q_ref[pair, step] for pair in range(per)]

    def scores(pair, index):
        keys = k_ref[pair, pl.ds(pl.multiple_of(index * chunk, chunk), chunk), :]
        return mm(keys, queries[pair])

    last = (step * block) // chunk
    allowed = allowed_at(last * chunk, step * block, chunk, block)
    carried = []
    for pair in range(per):
        masked = jnp.where(allowed, scores(pair, last), LOWEST)
        top = jnp.max(masked, axis=0, keepdims=True)
        weights = jnp.exp(masked - top)
        total = jnp.sum(weights, axis=0, keepdims=True)
        mixed = mm(v_ref[pair, last], weights.astype(BF16))
        carried += [top, total, mixed]

    def one(index, state):
        fresh = []
        for pair in range(per):
            top, total, mixed = state[3 * pair : 3 * pair + 3]
            here = scores(pair, index)
            new_top = jnp.maximum(top, jnp.max(here, axis=0, keepdims=True))
            weights = jnp.exp(here - new_top)
            factor = jnp.exp(top - new_top)
            total = total * factor + jnp.sum(weights, axis=0, keepdims=True)
            mixed = mixed * factor + mm(v_ref[pair, index], weights.astype(BF16))
            fresh += [new_top, total, mixed]
        return tuple(fresh)

    final = lax.fori_loop(0, last, one, tuple(carried))
    for pair in range(per):
        top, total, mixed = final[3 * pair : 3 * pair + 3]
        mixed = mixed / total
        lse_ref[0, pair : pair + 1, :] = top + jnp.log(total)
        for dst in range(block // tokens):
            piece = mixed[:, dst * tokens : (dst + 1) * tokens]
            lanes = slice(pair * tokens, (pair + 1) * tokens)
            outf_ref[dst, :, lanes] = piece
            out_ref[dst, :, lanes] = piece.astype(BF16)


def attend(query, kv, per, block=512, chunk=512):
    sources, _, lanes = query.shape
    tokens = lanes // per
    length = sources * tokens
    steps = length // block
    here = pl.BlockSpec((block // tokens, HEAD, lanes), lambda i: (i, 0, 0))
    return pl.pallas_call(
        functools.partial(attend_body, per, tokens, block, chunk),
        grid=(steps,),
        in_specs=[whole(query.shape), whole(kv.shape)],
        out_specs=[here, here, pl.BlockSpec((1, 8, block), lambda i: (i, 0, 0))],
        out_shape=[
            jax.ShapeDtypeStruct((sources, HEAD, lanes), BF16),
            jax.ShapeDtypeStruct((sources, HEAD, lanes), F32),
            jax.ShapeDtypeStruct((steps, 8, block), F32),
        ],
        scratch_shapes=[
            pltpu.VMEM((per, steps, HEAD, block), BF16),
            pltpu.VMEM((per, length, HEAD), BF16),
            pltpu.VMEM((per, length // chunk, HEAD, chunk), BF16),
        ],
        compiler_params=params(),
        cost_estimate=about(1),
        name="attend",
    )(query, kv)


def attend_back_body(
    per, tokens, block, chunk, query_ref, kv_ref, go_ref, of_ref, lse_ref, out_ref, qt_ref, q_ref, kt_ref, k_ref, v_ref,
    dk_ref, dv_ref,
):
    sources = query_ref.shape[0]
    step = pl.program_id(0)

    @pl.when(step == 0)
    def _():
        lay_out(query_ref, qt_ref, per, tokens, block, scale=HEAD**-0.5)
        lay_out(query_ref, q_ref, per, tokens, block, turned=True, scale=HEAD**-0.5)
        lay_out(kv_ref.at[:, 0], kt_ref, per, tokens, chunk, scale=HEAD**-0.5)
        lay_out(kv_ref.at[:, 0], k_ref, per, tokens, chunk, turned=True)
        lay_out(kv_ref.at[:, 1], v_ref, per, tokens, chunk, turned=True)
        dk_ref[...] = jnp.zeros_like(dk_ref)
        dv_ref[...] = jnp.zeros_like(dv_ref)

    inner = block // tokens
    grads, deltas, lses, turned_grads, turned_queries, queries = [], [], [], [], [], []
    for pair in range(per):
        lanes = slice(pair * tokens, (pair + 1) * tokens)
        grad = jnp.concatenate([go_ref[dst, :, lanes] for dst in range(inner)], axis=1)
        mixed = jnp.concatenate([of_ref[dst, :, lanes] for dst in range(inner)], axis=1)
        wide = grad.astype(F32)
        grads.append(grad)
        deltas.append(jnp.sum(wide * mixed, axis=0, keepdims=True))
        turned_grads.append(wide.T.astype(BF16))
        lses.append(lse_ref[0, pair : pair + 1, :])
        queries.append(qt_ref[pair, step])
        turned_queries.append(q_ref[pair, pl.ds(pl.multiple_of(step * block, block), block), :])

    def one(index, state, allowed):
        rows = pl.ds(pl.multiple_of(index * chunk, chunk), chunk)
        fresh = []
        for pair in range(per):
            weights = jnp.exp(mm(k_ref[pair, rows, :], queries[pair]) - lses[pair])
            if allowed is not None:
                weights = jnp.where(allowed, weights, 0.0)
            back = mm(v_ref[pair, rows, :], grads[pair])
            dscore = (weights * (back - deltas[pair])).astype(BF16)
            dv_ref[pair, rows, :] += mm(weights.astype(BF16), turned_grads[pair])
            dk_ref[pair, rows, :] += mm(dscore, turned_queries[pair])
            fresh.append(state[pair] + mm(kt_ref[pair, index], dscore))
        return tuple(fresh)

    last = (step * block) // chunk
    start = tuple(jnp.zeros((HEAD, block), F32) for _ in range(per))
    state = lax.fori_loop(0, last, lambda i, s: one(i, s, None), start)
    state = one(last, state, allowed_at(last * chunk, step * block, chunk, block))
    for pair in range(per):
        lanes = slice(pair * tokens, (pair + 1) * tokens)
        for dst in range(inner):
            out_ref[step * inner + dst, 0, :, lanes] = state[pair][
                :, dst * tokens : (dst + 1) * tokens
            ].astype(BF16)

    @pl.when(step == pl.num_programs(0) - 1)
    def _():
        for pair in range(per):
            lanes = slice(pair * tokens, (pair + 1) * tokens)
            for src in range(sources):
                rows = slice(src * tokens, (src + 1) * tokens)
                out_ref[src, 1, :, lanes] = dk_ref[pair, rows, :].T.astype(BF16)
                out_ref[src, 2, :, lanes] = dv_ref[pair, rows, :].T.astype(BF16)


def attend_back(query, kv, grad, mixed, lse, per, chunk=512):
    sources, _, lanes = query.shape
    tokens = lanes // per
    length = sources * tokens
    steps, _, block = lse.shape
    here = pl.BlockSpec((block // tokens, HEAD, lanes), lambda i: (i, 0, 0))
    shape = (sources, 3, HEAD, lanes)
    return pl.pallas_call(
        functools.partial(attend_back_body, per, tokens, block, chunk),
        grid=(steps,),
        in_specs=[
            whole(query.shape), whole(kv.shape), here, here, pl.BlockSpec((1, 8, block), lambda i: (i, 0, 0)),
        ],
        out_specs=whole(shape),
        out_shape=jax.ShapeDtypeStruct(shape, BF16),
        scratch_shapes=[
            pltpu.VMEM((per, steps, HEAD, block), BF16),
            pltpu.VMEM((per, length, HEAD), BF16),
            pltpu.VMEM((per, length // chunk, HEAD, chunk), BF16),
            pltpu.VMEM((per, length, HEAD), BF16),
            pltpu.VMEM((per, length, HEAD), BF16),
            pltpu.VMEM((per, length, HEAD), F32),
            pltpu.VMEM((per, length, HEAD), F32),
        ],
        compiler_params=params(),
        cost_estimate=about(1),
        name="attend_back",
    )(query, kv, grad, mixed, lse)


def merge_body(place, x_ref, ot_ref, mine_ref, theirs_ref, mo_ref, mn_ref, mf_ref, x1_ref, h_ref, o_ref):
    at, core = place[0], place[1]
    starts = piece_starts(at, core, mo_ref.shape[0])
    o_ref[...] = ot_ref[...].astype(F32).T.astype(BF16)
    merged = full_row(at, mine_ref, theirs_ref, BIAS_MERGE)
    for (begin, size), weight in zip(starts, (mo_ref, mn_ref, mf_ref)):
        merged = merged + mm(o_ref[:, pl.ds(begin, size)], weight[...])
    x1 = x_ref[...].astype(F32) + merged
    x1_ref[...] = x1
    unit, _ = normalise(x1)
    gain = full_row(at, mine_ref, theirs_ref, GAIN_MLP)
    shift = full_row(at, mine_ref, theirs_ref, SHIFT_MLP)
    h_ref[...] = (unit * gain + shift).astype(BF16)


def merge(place, x, ot, mine, theirs, weights):
    shape = x.shape
    operands = (x, ot, mine, theirs, *weights)
    return pl.pallas_call(
        merge_body,
        grid_spec=pltpu.PrefetchScalarGridSpec(
            num_scalar_prefetch=1,
            grid=(1,),
            in_specs=[whole(member.shape) for member in operands],
            out_specs=[whole(shape)] * 3,
        ),
        out_shape=[
            jax.ShapeDtypeStruct(shape, F32),
            jax.ShapeDtypeStruct(shape, BF16),
            jax.ShapeDtypeStruct(shape, BF16),
        ],
        compiler_params=params(),
        cost_estimate=about(1),
        name="merge",
    )(place, *operands)


def gelu_pair(inner):
    square = inner * inner
    bend = jnp.tanh(GELU_A * (inner + GELU_B * (inner * square)))
    active = 0.5 * inner * (1.0 + bend)
    slope = 0.5 * (1.0 + bend) + 0.5 * inner * (1.0 - bend * bend) * (GELU_A * (1.0 + 3.0 * GELU_B * square))
    return active, slope


def read_expand_bias(at, mine_ref, theirs_ref, bias_ref):
    count, wide = bias_ref.shape
    count = count // 2
    beside = mine_ref.shape[1] // wide
    for row in range(count):
        line = BIAS_EXPAND // 2 + row // beside
        lanes = slice(row % beside * wide, (row % beside + 1) * wide)
        mine = mine_ref[line : line + 1, lanes].astype(F32)
        theirs = theirs_ref[line : line + 1, lanes].astype(F32)
        bias_ref[row : row + 1, :] = jnp.where(at == 0, mine, theirs)
        bias_ref[count + row : count + row + 1, :] = jnp.where(at == 0, theirs, mine)


def mlp_body(
    place, x1_ref, h_ref, dy_ref, mine_ref, theirs_ref, mo_ref, mn_ref, mf_ref, eo_ref, en0_ref, en1_ref, ef0_ref,
    ef1_ref, own_ref, rest_ref, out_ref, dx_ref, da_ref, dot_ref, total_ref, dh_ref, bias_ref, sums_ref,
):
    at, core = place[0], place[1]
    step = pl.program_id(0)
    starts = piece_starts(at, core, mo_ref.shape[0])
    wide = eo_ref.shape[1]
    width = sums_ref.shape[1]
    beside = width // wide

    @pl.when(step == 0)
    def _():
        total_ref[...] = jnp.zeros_like(total_ref)
        dh_ref[...] = jnp.zeros_like(dh_ref)
        sums_ref[...] = jnp.zeros_like(sums_ref)
        read_expand_bias(at, mine_ref, theirs_ref, bias_ref)

    contract = contract_block(step, pl.num_programs(0), at, own_ref, rest_ref)
    expand = expand_pieces(step, pl.num_programs(0), eo_ref, en0_ref, en1_ref, ef0_ref, ef1_ref)
    inner = bias_ref[pl.ds(step, 1), :]
    for (begin, size), weight in zip(starts, expand):
        inner = inner + mm(h_ref[:, pl.ds(begin, size)], weight)
    active, slope = gelu_pair(inner)
    total_ref[...] += mm(active.astype(BF16), contract)
    grad = (mm_nt(dy_ref[...], contract) * slope).astype(BF16)
    sums_ref[
        pl.ds(SUM_EXPAND + step // beside, 1), pl.ds(pl.multiple_of(step % beside * wide, wide), wide)
    ] = jnp.sum(grad.astype(F32), axis=0, keepdims=True)
    for (begin, size), weight in zip(starts, expand):
        dh_ref[:, pl.ds(begin, size)] += mm_nt(grad, weight)

    @pl.when(step == pl.num_programs(0) - 1)
    def _():
        x1 = x1_ref[...]
        bias = full_row(at, mine_ref, theirs_ref, BIAS_CONTRACT)
        out_ref[...] = (x1 + total_ref[...] + bias).astype(BF16)
        gain = full_row(at, mine_ref, theirs_ref, GAIN_MLP)
        unit, inverse = normalise(x1)
        grad = dh_ref[...]
        dy = dy_ref[...].astype(F32)
        dx = dy + normalise_back(grad, unit, inverse, gain)
        dx_ref[...] = dx
        da = dx.astype(BF16)
        rows = da.shape[0]
        da_ref[:rows, :] = da
        sums_ref[0:1, :] = jnp.sum(dy, axis=0, keepdims=True)
        sums_ref[1:2, :] = jnp.sum(grad * unit, axis=0, keepdims=True)
        sums_ref[2:3, :] = jnp.sum(grad, axis=0, keepdims=True)
        sums_ref[3:4, :] = jnp.sum(da.astype(F32), axis=0, keepdims=True)
        da_ref[rows:, :] = sums_ref[...].astype(BF16)
        for (begin, size), weight in zip(starts, (mo_ref, mn_ref, mf_ref)):
            dot_ref[pl.ds(begin, size), :] = mm_nt(weight[...], da).astype(BF16)


def expand_pieces(block, blocks, own, near_low, near_high, far_low, far_high):
    low = block < blocks // 2
    return (
        own[...],
        jnp.where(low, near_low[...], near_high[...]),
        jnp.where(low, far_low[...], far_high[...]),
    )


def hidden_specs(expand, contract, wide, block_of):
    own = expand[0].shape[1] // wide
    each = expand[1].shape[1] // wide
    own_contract, rest = contract
    _, shard, width = rest.shape
    held = wide // shard
    specs = [pl.BlockSpec((expand[0].shape[0], wide), lambda i, s: (0, block_of(i, s)))]
    for index in range(1, 5):
        first = (index - 1) % 2 * each
        specs.append(
            pl.BlockSpec(
                (expand[index].shape[0], wide),
                lambda i, s, first=first: (0, jnp.clip(block_of(i, s) - first, 0, each - 1)),
            )
        )
    blocks = own // 2
    specs.append(
        pl.BlockSpec((wide, width), lambda i, s: (jnp.clip(block_of(i, s) - s[0] * blocks, 0, blocks - 1), 0))
    )
    specs.append(
        pl.BlockSpec(
            (held, shard, width), lambda i, s: (jnp.clip(block_of(i, s) - (1 - s[0]) * blocks, 0, blocks - 1), 0, 0)
        )
    )
    return specs


def contract_block(block, blocks, at, own_ref, rest_ref):
    wide, width = own_ref.shape
    return jnp.where(block // (blocks // 2) == at, own_ref[...], rest_ref[...].reshape(wide, width))


def mlp(place, x1, normed, dy, mine, theirs, merge_w, expand, contract):
    rows, width = x1.shape
    wide = 512
    steps = expand[0].shape[1] // wide
    sums = -(-(SUM_EXPAND + steps * wide // width) // 16) * 16
    operands = (x1, normed, dy, mine, theirs, *merge_w)
    in_specs = [whole(member.shape) for member in operands]
    in_specs += hidden_specs(expand, contract, wide, lambda i, _: i)
    shapes = [
        ((rows, width), BF16),
        ((rows, width), F32),
        ((rows + sums, width), BF16),
        ((width, rows), BF16),
    ]
    return pl.pallas_call(
        mlp_body,
        grid_spec=pltpu.PrefetchScalarGridSpec(
            num_scalar_prefetch=1,
            grid=(steps,),
            in_specs=in_specs,
            out_specs=[whole(shape) for shape, _ in shapes],
            scratch_shapes=[
                pltpu.VMEM((rows, width), F32),
                pltpu.VMEM((rows, width), F32),
                pltpu.VMEM((steps, wide), F32),
                pltpu.VMEM((sums, width), F32),
            ],
        ),
        out_shape=[jax.ShapeDtypeStruct(shape, dtype) for shape, dtype in shapes],
        compiler_params=params(),
        cost_estimate=about(1),
        name="mlp",
    )(place, *operands, *expand, *contract)


def hidden_part(step, at, core, own_steps):
    part = own_steps // 2
    return jnp.where(
        step < part, at * own_steps + core * part + step, (1 - at) * own_steps + core * part + step - part
    )


def tail_rows(merge_rows):
    return -(-(merge_rows + 2) // 16) * 16


def weights_body(own_steps, place, *refs):
    h_refs, dy_refs = refs[:4], refs[4:8]
    mine_ref, theirs_ref, eo_ref, en0_ref, en1_ref, ef0_ref, ef1_ref, own_ref, rest_ref = refs[8:17]
    contract_ref, out_ref, bias_ref, h_ref, turned_ref, dy_ref, act_ref, du_ref = refs[17:]
    at, core = place[0], place[1]
    step = pl.program_id(0)
    part = own_steps // 2
    half = eo_ref.shape[0]
    starts = piece_starts(at, core, half)
    block = hidden_part(step, at, core, own_steps)
    wide = eo_ref.shape[1]
    chips, _, width = out_ref.shape
    expand_rows = half // chips
    rows = h_refs[0].shape[0]
    some = 2 * rows

    @pl.when(step == 0)
    def _():
        read_expand_bias(at, mine_ref, theirs_ref, bias_ref)
        for index in range(4):
            here = slice(index * rows, (index + 1) * rows)
            h_ref[here, :] = h_refs[index][...]
            dy_ref[here, :] = dy_refs[index][...]
            mine = h_refs[index][:, pl.ds(pl.multiple_of(at * half, half), half)]
            turned_ref[:, here] = mine.astype(F32).T.astype(BF16)

    def work(forward):
        contract = contract_block(block, 2 * own_steps, at, own_ref, rest_ref)
        expand = expand_pieces(block, 2 * own_steps, eo_ref, en0_ref, en1_ref, ef0_ref, ef1_ref)
        for index in range(4 * rows // some):
            here = slice(index * some, (index + 1) * some)
            inner = bias_ref[pl.ds(block, 1), :]
            for (begin, size), weight in zip(starts, expand):
                inner = inner + mm(h_ref[here, pl.ds(begin, size)], weight)
            active, slope = gelu_pair(inner)
            if forward:
                act_ref[here, :] = active.astype(BF16)
            du_ref[here, :] = (mm_nt(dy_ref[here, :], contract) * slope).astype(BF16)
        return mm(turned_ref[...], du_ref[...]).astype(BF16)

    def store_expand(value, turn, column):
        own = pl.ds(pl.multiple_of(turn * expand_rows, expand_rows), expand_rows)
        for chip in range(chips):
            out_ref[chip, own, column * wide : (column + 1) * wide] = value[
                chip * expand_rows : (chip + 1) * expand_rows, :
            ]

    for now in range(part):

        @pl.when(step == now)
        def _():
            store_expand(work(True), at, now)
            contract_ref[now * wide : (now + 1) * wide, :] = mm_tn(act_ref[...], dy_ref[...]).astype(BF16)

        @pl.when(step == part + now)
        def _():
            store_expand(work(False), 1 - at, now)


def mlp_weights(place, chips, normed, dy, mine, theirs, expand, contract):
    rows, width = dy[0].shape
    wide = 512
    half = expand[0].shape[0]
    own_steps = expand[0].shape[1] // wide // 2
    part = own_steps // 2
    operands = (*normed, *dy, mine, theirs)
    in_specs = [whole(member.shape) for member in operands]
    in_specs += hidden_specs(expand, contract, wide, lambda i, s: hidden_part(i, s[0], s[1], own_steps))
    shapes = [(part * wide, width), (chips, 2 * (half // chips), width)]
    return pl.pallas_call(
        functools.partial(weights_body, own_steps),
        grid_spec=pltpu.PrefetchScalarGridSpec(
            num_scalar_prefetch=1,
            grid=(own_steps,),
            in_specs=in_specs,
            out_specs=[whole(shape) for shape in shapes],
            scratch_shapes=[
                pltpu.VMEM((2 * own_steps, wide), F32),
                pltpu.VMEM((4 * rows, width), BF16),
                pltpu.VMEM((half, 4 * rows), BF16),
                pltpu.VMEM((4 * rows, width), BF16),
                pltpu.VMEM((4 * rows, wide), BF16),
                pltpu.VMEM((4 * rows, wide), BF16),
            ],
        ),
        out_shape=[jax.ShapeDtypeStruct(shape, BF16) for shape in shapes],
        compiler_params=params(),
        cost_estimate=about(1),
        name="mlp_weights",
    )(place, *operands, *expand, *contract)


def merge_weights_body(hidden, place, *refs):
    o_refs, da_refs, out_ref = refs[:4], refs[4:8], refs[8]
    at, core = place[0], place[1]
    chips, tail, width = out_ref.shape
    half = width // 2
    tokens = o_refs[0].shape[0]
    total, sums = 0.0, 0.0
    for o_ref, da_ref in zip(o_refs, da_refs):
        total = total + mm_tn(o_ref[...], da_ref[:tokens, :])
        sums = sums + da_ref[tokens:, :].astype(F32)
    rows = total.shape[0] // chips
    for chip in range(chips):
        out_ref[chip, :rows, :] = total[chip * rows : (chip + 1) * rows, :].astype(BF16)
    out_ref[:, rows:, :] = jnp.zeros((chips, tail - rows, width), BF16)
    own = jnp.where(at == 0, sums[:, :half], sums[:, half:])
    own_hidden = jnp.where(at == 0, sums[SUM_EXPAND : SUM_EXPAND + hidden], sums[SUM_EXPAND + hidden : SUM_EXPAND + 2 * hidden])
    for row in range(2):
        vector = jnp.concatenate([own[2 * row : 2 * row + 1], own[2 * row + 1 : 2 * row + 2]], axis=1)
        vector = jnp.where(core == 0, vector, own_hidden[row : row + 1])
        out_ref[0, rows + row : rows + row + 1, :] = vector.astype(BF16)


def merge_weights(place, chips, mixed, grad, hidden):
    rows, width = mixed[0].shape
    quarter = mixed[1].shape[1]
    shape = (chips, tail_rows(quarter // chips), width)
    return pl.pallas_call(
        functools.partial(merge_weights_body, hidden // width // 2),
        grid_spec=pltpu.PrefetchScalarGridSpec(
            num_scalar_prefetch=1,
            grid=(1,),
            in_specs=[pl.BlockSpec((rows, quarter), lambda i, s: (0, 2 * s[0] + s[1]))]
            + [whole((rows, quarter))] * 3
            + [whole(grad[0].shape)] * 4,
            out_specs=whole(shape),
        ),
        out_shape=jax.ShapeDtypeStruct(shape, BF16),
        compiler_params=params(),
        cost_estimate=about(1),
        name="merge_weights",
    )(place, *mixed, *grad)


def spread_expand_body(in_ref, out_ref):
    rows, columns = out_ref.shape
    width = columns // 4
    for core in range(2):
        for part in range(2):
            column = (2 * part + core) * width
            out_ref[:, column : column + width] = in_ref[core, part * rows : (part + 1) * rows, :].astype(F32)


def spread_expand(gathered, shape):
    devices, rows, width = gathered.shape
    chips = devices // 2
    return pl.pallas_call(
        spread_expand_body,
        grid=(chips,),
        in_specs=[pl.BlockSpec((2, rows, width), lambda i: (i, 0, 0))],
        out_specs=pl.BlockSpec((shape[0] // chips, shape[1]), lambda i: (i, 0)),
        out_shape=jax.ShapeDtypeStruct(shape, F32),
        compiler_params=params(),
        cost_estimate=about(1),
        name="spread_expand",
    )(gathered)


def spread_contract_body(place, *refs):
    out_ref = refs[4]
    phase = 2 * pl.program_id(0) + pl.program_id(1)
    for index in range(4):

        @pl.when(phase == index)
        def _():
            out_ref[...] = refs[index][...].reshape(out_ref.shape).astype(F32)


def spread_contract(place, stacks, shape):
    ring, rows, width = stacks[0].shape

    def source(index):
        def block(i, j, k, s):
            phase = 2 * i + j
            slot = jnp.where(phase < index, 0, jnp.where(phase > index, ring - 1, k))
            return ((s[3] - slot + ring) % ring, 0, 0)

        return pl.BlockSpec((1, rows, width), block)

    def target(i, j, k, s):
        return (((i + s[1]) % 2 * 2 + (j + s[2]) % 2) * ring + k, 0)

    return pl.pallas_call(
        spread_contract_body,
        grid_spec=pltpu.PrefetchScalarGridSpec(
            num_scalar_prefetch=1,
            grid=(2, 2, ring),
            in_specs=[source(index) for index in range(4)],
            out_specs=pl.BlockSpec((rows, width), target),
        ),
        out_shape=jax.ShapeDtypeStruct(shape, F32),
        compiler_params=params(),
        cost_estimate=about(1),
        name="spread_contract",
    )(place, *stacks)


def heads_body(dp_ref, h_ref, out_ref):
    @pl.when(pl.program_id(0) == 0)
    def _():
        out_ref[...] = jnp.zeros_like(out_ref)

    _, parts, head, lanes = dp_ref.shape
    out_ref[...] += mm(dp_ref[0].reshape(parts * head, lanes), h_ref[0])


def heads_gradient(dp, normed):
    sources, parts, head, lanes = dp.shape
    width = normed.shape[2]
    return pl.pallas_call(
        heads_body,
        grid=(sources,),
        in_specs=[
            pl.BlockSpec((1, parts, head, lanes), lambda i: (i, 0, 0, 0)),
            pl.BlockSpec((1, lanes, width), lambda i: (i, 0, 0)),
        ],
        out_specs=whole((parts * head, width)),
        out_shape=jax.ShapeDtypeStruct((parts * head, width), F32),
        compiler_params=params(),
        cost_estimate=about(1),
        name="heads_gradient",
    )(dp, normed)


def spread_heads_body(begin, in_ref, heads_ref, merge_ref):
    heads, _, width = in_ref.shape
    half = width // 2
    rows = 3 * HEAD // 2
    some = 4
    for part in range(3):
        for first in range(0, heads, some):
            turned = []
            for head in range(first, first + some):
                for row in range(part * HEAD, (part + 1) * HEAD, 32):
                    side = row // rows
                    here = row - side * rows
                    turned.append(in_ref[head, here : here + 32, side * half : (side + 1) * half])
            piece = jnp.concatenate([member.astype(F32) for member in turned], axis=0)
            column = (part * heads + first) * HEAD
            heads_ref[:, column : column + some * HEAD] = piece.T
    if merge_ref is not None:
        spread_merge_body(begin, in_ref, merge_ref)


def spread_merge_body(begin, in_ref, merge_ref):
    _, chips, rows, _ = merge_ref.shape
    for chip in range(chips):
        for core in range(2):
            merge_ref[core, chip] = in_ref[2 * chip + core, begin : begin + rows, :].astype(F32)


def spread_heads(gathered, begin, shape, merge_shape):
    devices, _, width = gathered.shape
    chunked = (2, devices // 2, merge_shape[0] // devices, width)
    heads, merged = pl.pallas_call(
        functools.partial(spread_heads_body, begin),
        grid=(1,),
        in_specs=[whole(gathered.shape)],
        out_specs=[whole(shape), whole(chunked)],
        out_shape=[jax.ShapeDtypeStruct(shape, F32), jax.ShapeDtypeStruct(chunked, F32)],
        compiler_params=params(),
        cost_estimate=about(1),
        name="spread_heads",
    )(gathered)
    return heads, merged.reshape(merge_shape)


def back_body(
    place, dp_ref, x_ref, dx_ref, mine_ref, theirs_ref, own_ref, qn_ref, qf_ref, rn_ref, rf_ref, out_ref, sums_ref, dh_ref
):
    at, core = place[0], place[1]
    part = pl.program_id(0)
    starts = piece_starts(at, core, own_ref.shape[0])
    heads, _, head, rows = dp_ref.shape

    @pl.when(part == 0)
    def _():
        dh_ref[...] = jnp.zeros_like(dh_ref)
        sums_ref[...] = jnp.zeros_like(sums_ref)

    def work(weights):
        grad = dp_ref[...].reshape(heads * head, rows)
        for (begin, size), weight in zip(starts, weights):
            dh_ref[pl.ds(begin, size), :] += mm(weight[...], grad)
        return mm_nt(jnp.ones((8, rows), BF16), grad)[0:1, :]

    @pl.when(part == 0)
    def _():
        sums_ref[2:3, :] = work((own_ref, qn_ref, qf_ref))

    @pl.when(part == 1)
    def _():
        work((own_ref, rn_ref, rf_ref))

    @pl.when(part == 2)
    def _():
        sums_ref[3:4, :] = work((own_ref, rn_ref, rf_ref))
        dh = dh_ref[...].T
        unit, inverse = normalise(x_ref[...].astype(F32))
        gain = full_row(at, mine_ref, theirs_ref, GAIN_ATTN)
        out_ref[...] = dx_ref[...] + normalise_back(dh, unit, inverse, gain)
        sums_ref[0:1, :] = jnp.sum(dh * unit, axis=0, keepdims=True)
        sums_ref[1:2, :] = jnp.sum(dh, axis=0, keepdims=True)


def back(place, dp, x, dx, mine, theirs, own, query_w, rest_w):
    rows, width = x.shape
    heads, parts, head, _ = dp.shape
    vectors = (x, dx, mine, theirs)
    return pl.pallas_call(
        back_body,
        grid_spec=pltpu.PrefetchScalarGridSpec(
            num_scalar_prefetch=1,
            grid=(parts,),
            in_specs=[pl.BlockSpec((heads, 1, head, rows), lambda t, _: (0, t, 0, 0))]
            + [whole(member.shape) for member in vectors]
            + [pl.BlockSpec((own.shape[0], width), lambda t, _: (0, t))]
            + [whole(member.shape) for member in query_w]
            + [pl.BlockSpec((member.shape[0], width), lambda t, _: (0, jnp.maximum(t - 1, 0))) for member in rest_w],
            out_specs=[whole((rows, width)), whole((8, width))],
            scratch_shapes=[pltpu.VMEM((width, rows), F32)],
        ),
        out_shape=[
            jax.ShapeDtypeStruct((rows, width), F32),
            jax.ShapeDtypeStruct((8, width), F32),
        ],
        compiler_params=params(),
        cost_estimate=about(1),
        name="back",
    )(place, dp, *vectors, own, *query_w, *rest_w)


def after(value, *others):
    return lax.optimization_barrier((value,) + others)[0]


def per_device(
    mesh_sizes, tokens_in, gain_attn, shift_attn, w_heads, bias_query, bias_value, w_merge, bias_merge, gain_mlp, shift_mlp,
    w_expand, bias_expand, w_contract, bias_contract, cotangent,
):
    nctx = mesh_sizes[0]
    seqs, tokens, width = tokens_in.shape
    rows = seqs * tokens
    half = width // 2
    heads = width // HEAD
    hidden = w_expand.shape[1]
    pairs = seqs * heads
    same = max(1, nctx // pairs)
    per = max(1, pairs // nctx)
    groups = seqs // per
    ctx = lax.axis_index("ctx")
    at = lax.axis_index("fsdp")
    core = ctx % 2
    line, ring_at, ring = ctx // 2 % 2, ctx // 4, nctx // 4
    place = jnp.stack([at, core, line, ring_at, ctx]).astype(jnp.int32)

    def over_x(value):
        return lax.ppermute(value, "fsdp", [(0, 1), (1, 0)])

    def over_core(value):
        return lax.ppermute(value, "ctx", [(i, i ^ 1) for i in range(nctx)])

    def over_line(value):
        return lax.ppermute(value, "ctx", [(i, i ^ 2) for i in range(nctx)])

    def on_ring(value, by):
        return lax.ppermute(value, "ctx", [(i, (i + 4 * by) % nctx) for i in range(nctx)])

    def over_both(value):
        size = mesh_sizes[1]
        swap = [(i * size + j, (i ^ 1) * size + 1 - j) for i in range(nctx) for j in range(size)]
        return lax.ppermute(value, ("ctx", "fsdp"), swap)

    def exchange(value):
        return lax.all_to_all(value, "ctx", 0, 0)

    def to_send(value):
        lead = value.shape[1:-1]
        value = value.reshape((heads,) + lead + (groups, per * tokens))
        value = jnp.moveaxis(value, -2, 1).reshape((nctx // same,) + lead + (per * tokens,))
        return value if same == 1 else jnp.repeat(value, same, axis=0)

    def received(value):
        value = value[::same]
        lead = value.shape[1:-1]
        value = value.reshape((heads, groups) + lead + (per * tokens,))
        return jnp.moveaxis(value, 1, -2).reshape((heads,) + lead + (rows,))

    def quarter_of(weight, first, count):
        size = weight.shape[0] // 2
        return lax.dynamic_slice(weight, (core * size, first), (size, count))

    def halves(value):
        mine = lax.dynamic_index_in_dim(value, at, 0, keepdims=False)
        return mine + over_x(lax.dynamic_index_in_dim(value, 1 - at, 0, keepdims=False))

    vectors = (gain_attn, shift_attn, bias_query, bias_value, bias_merge, gain_mlp, shift_mlp, bias_contract, bias_expand)
    shard = w_contract.shape[0] // nctx
    first, mine = parcel(place, w_heads, w_contract, vectors, shard)
    first_near = over_x(first)
    rest_piece, first_near = lax.optimization_barrier((quarter_of(w_heads, width, 2 * width), first_near))
    query_near = first_near[: half // 2]
    theirs = first_near[half // 2 + shard :]
    contract = (w_contract, lax.all_gather(first_near[half // 2 : half // 2 + shard], "ctx", axis=0))
    query_w = (query_near, over_core(query_near))
    rest_near = over_x(rest_piece)
    merge_near = over_x(after(quarter_of(w_merge, 0, width), rest_near))
    expand_low = over_x(after(quarter_of(w_expand, 0, hidden // 2), rest_near))
    expand_high = over_x(after(quarter_of(w_expand, hidden // 2, hidden // 2), expand_low))

    x = tokens_in.reshape(rows, width)
    dy = cotangent.reshape(rows, width)
    dy_x = over_x(after(dy, expand_high))

    query_rows, normed = front_query(place, x, mine, theirs, w_heads, *query_w)
    query = exchange(to_send(query_rows))
    rest_w = (rest_near, over_core(after(rest_near, query)))
    kv = exchange(to_send(front_rest(place, after(normed, query), mine, theirs, w_heads, *rest_w)))
    normed_all = lax.all_gather(normed, "ctx", axis=0, tiled=False)
    mixed_b, mixed_f, lse = attend(query, kv, per)
    merge_w = (w_merge, merge_near, over_core(after(merge_near, kv)))
    expand_w = (
        w_expand, expand_low, expand_high, over_core(after(expand_low, kv)), over_core(after(expand_high, lse)),
    )
    mixed = received(exchange(mixed_b)).reshape(width, rows)
    x1, normed_two, mixed_rows = merge(place, x, mixed, mine, theirs, merge_w)

    def of_four(value, there):
        return value, there, over_core(value), over_core(there)

    def all_four(value):
        return value, over_x(value), over_core(value), over_both(value)

    def quarter_at(value, at, core):
        return lax.dynamic_slice_in_dim(value, (2 * at + core) * (width // 4), width // 4, 1)

    dy_four = of_four(after(dy, mixed), after(dy_x, mixed))
    normed_four = of_four(normed_two, over_x(normed_two))
    grad_contract, grad_expand = mlp_weights(
        place, nctx // 2, normed_four, dy_four, mine, theirs, expand_w, contract
    )
    chips = [[2 * chip + one for chip in range(nctx // 2)] for one in range(2)]
    grad_contract = grad_contract.reshape(2, ring, -1, width)
    to_line = lax.dynamic_index_in_dim(grad_contract, 1 - line, 0, keepdims=False)
    x1, to_line, grad_expand, normed_all = lax.optimization_barrier((x1, to_line, grad_expand, normed_all))
    reduced = lax.psum_scatter(grad_expand, "ctx", scatter_dimension=0, axis_index_groups=chips)
    contract_line = over_line(to_line)
    block_out, dx1, da, grad_mixed = mlp(
        place, x1, normed_two, dy, mine, theirs, merge_w, expand_w, contract
    )
    grad_out = exchange(to_send(grad_mixed.reshape(heads, HEAD, rows)))

    contract_half = lax.dynamic_index_in_dim(grad_contract, line, 0, keepdims=False).astype(F32)
    contract_half = (contract_half + after(contract_line, da).astype(F32)).astype(BF16)

    def chunk_of(by):
        return lax.dynamic_index_in_dim(contract_half, (ring_at + by) % ring, 0, keepdims=False)

    contract_parts = [on_ring(chunk_of(by), by) for by in range(1, ring)]

    mixed_four = (
        mixed_rows,
        over_x(quarter_at(mixed_rows, 1 - at, core)),
        over_core(quarter_at(mixed_rows, at, 1 - core)),
        over_both(quarter_at(mixed_rows, 1 - at, 1 - core)),
    )
    mixed_four = lax.optimization_barrier((mixed_four, da))[0]
    grads_four = of_four(da, over_x(da))
    grads_four, contract_half = lax.optimization_barrier((grads_four, contract_half))
    grad_merge = merge_weights(place, nctx // 2, mixed_four, grads_four, hidden)
    contract_sum = chunk_of(0).astype(F32)
    contract_parts, grad_merge = lax.optimization_barrier((contract_parts, grad_merge))
    for part in contract_parts:
        contract_sum = contract_sum + part.astype(F32)
    contract_sum = contract_sum.astype(BF16)
    grad_merge, grad_out, contract_sum = lax.optimization_barrier((grad_merge, grad_out, contract_sum))
    grad_merge = grad_merge.reshape((ring, 2) + grad_merge.shape[1:])
    merge_line = over_line(lax.dynamic_index_in_dim(grad_merge, 1 - line, 1, keepdims=False))

    dqkv = attend_back(query, kv, grad_out, mixed_f, lse, per)
    dp = received(exchange(dqkv))

    own_line = [on_ring(contract_sum, by) for by in range(1, ring)]
    own_line, dqkv = lax.optimization_barrier((own_line, dqkv))
    grad_expand = lax.all_gather(after(reduced, dqkv), "ctx", axis=0)
    own_line = jnp.stack([contract_sum] + own_line)
    other_line = over_line(own_line)
    merge_half = lax.dynamic_index_in_dim(grad_merge, line, 1, keepdims=False).astype(F32)
    merge_half = (merge_half + after(merge_line, dqkv).astype(F32)).astype(BF16)
    merge_parts = [
        on_ring(lax.dynamic_index_in_dim(merge_half, (ring_at + by) % ring, 0, keepdims=False), by)
        for by in range(1, ring)
    ]

    if groups > 1:
        normed_all = lax.dynamic_slice_in_dim(normed_all, (ctx // same % groups) * tokens * per, tokens * per, 1)
    grad_heads = heads_gradient(dqkv, normed_all)
    merge_parts = lax.optimization_barrier((merge_parts, grad_heads))[0]
    if groups > 1:
        members = [
            [first + one + same * group for group in range(groups)]
            for first in range(0, nctx, groups * same)
            for one in range(same)
        ]
        grad_heads = lax.psum(grad_heads, "ctx", axis_index_groups=members)
    kept = lax.dynamic_slice_in_dim(grad_heads, at * half, half, 1)
    sent = lax.dynamic_slice_in_dim(grad_heads, (1 - at) * half, half, 1)
    kept = (kept + over_x(sent.astype(BF16)).astype(F32)).astype(BF16)
    if groups * same > 1:
        share = kept.shape[0] // (groups * same)
        kept = lax.dynamic_slice_in_dim(kept, ctx % (groups * same) * share, share, 0)
    rows_here = kept.shape[0] // 2
    kept = jnp.concatenate([kept[:rows_here], kept[rows_here:]], axis=1)
    kept = jnp.pad(kept, ((0, -rows_here % 16), (0, 0)))
    own_merge = lax.dynamic_index_in_dim(merge_half, ring_at, 0, keepdims=False).astype(F32)
    for part in merge_parts:
        own_merge = own_merge + part.astype(F32)
    own_merge = own_merge.astype(BF16)
    spread = jnp.concatenate([kept, own_merge])
    spread, other_line, dp, grad_expand = lax.optimization_barrier((spread, other_line, dp, grad_expand))
    expand_sum = spread_expand(grad_expand, w_expand.shape)
    spread = lax.all_gather(spread, "ctx", axis=0, tiled=False)
    stacks = (own_line, other_line, over_core(own_line), over_core(other_line))
    contract_sum = spread_contract(place, stacks, w_contract.shape)
    begin = kept.shape[0]
    merge_rows = half // nctx
    first = begin + merge_rows
    vectors = spread[:2, first : first + 2].astype(F32)
    if groups * same == 1:
        heads_sum, merge_sum = spread_heads(spread, begin, w_heads.shape, w_merge.shape)
    else:
        by_head = spread[:, :rows_here].reshape(nctx, rows_here, 2, half)
        by_head = jnp.swapaxes(by_head, 1, 2).reshape(heads, 2, -1, half)
        by_head = jnp.swapaxes(by_head, 1, 2).reshape(heads, -1, width)
        merge_sum = spread[:, begin:first].reshape(nctx // 2, 2, merge_rows, width)
        merge_sum = jnp.swapaxes(merge_sum, 0, 1).reshape(heads, -1, width)
        heads_sum, merge_sum = spread_heads(
            jnp.concatenate([by_head, merge_sum], axis=1), by_head.shape[1], w_heads.shape, w_merge.shape
        )

    grad_tokens, sums_attn = back(place, dp, x, dx1, mine, theirs, w_heads, query_w, rest_w)
    last = halves(sums_attn[:4].reshape(4, 2, half).swapaxes(0, 1))
    last = jnp.sum(exchange(jnp.broadcast_to(last, (nctx,) + last.shape)), axis=0)
    return (
        block_out.reshape(tokens_in.shape),
        grad_tokens.reshape(tokens_in.shape),
        last[0],
        last[1],
        heads_sum,
        last[2],
        last[3],
        merge_sum,
        vectors[0, 1, half:],
        vectors[0, 0, half:],
        vectors[0, 1, :half],
        expand_sum,
        vectors[1].reshape(-1),
        contract_sum,
        vectors[0, 0, :half],
    )


def solution(mesh):
    rows, vec, mat = P("fsdp", "ctx", None), P("fsdp"), P("fsdp", None)
    return jax.shard_map(
        functools.partial(per_device, (mesh.shape["ctx"], mesh.shape["fsdp"])),
        mesh=mesh,
        in_specs=(rows, vec, vec, mat, vec, vec, mat, vec, vec, vec, mat, vec, mat, vec, rows),
        out_specs=(rows, rows, vec, vec, mat, vec, vec, mat, vec, vec, vec, mat, vec, mat, vec),
        check_vma=False,
    )
```

profile of v0, /device:TPU:0, one launch (start us, length us, event | category | flops | bytes accessed | tf_op | source)
XLA Modules:
  0.0 461.1 jit_solution(17612704518529114802)
XLA Ops:
  7.9 2.9 parcel.1
  10.7 2.9 collective-permute-start
  13.7 2.3 constant_dynamic-slice_fusion.8
  16.0 16.1 %collective-permute-done = bf16[400,1024]{1,0:T(8,128)(2,1)S(1)} collective-permute-done((bf16[400,1024]{1,0:T(8,128)(2,1)}, bf16[400,1024]{1,0:T(8,128)(2,1)S(1)}, u32[]{:S(2)}, u32[]{:S(2)}) %collective-permute-start) | collective-permute-done | bytes 819232 | tf_op jit(solution)/shard_map/ppermute | solution.py:978
  35.8 5.6 %front_query.1 = (bf16[16,64,256]{2,1,0:T(8,128)(2,1)}, bf16[256,1024]{1,0:T(8,128)(2,1)}) custom-call(s32[5]{0:T(128)} %stack.38.place, bf16[256,1024]{1,0:T(8,128)(2,1)} %bitcast.81, bf16[16,1024]{1,0:T(8,128)(2,1)} %get-tuple-element.82.mine_ref.refs_8_, bf16[16,1024]{1,0:T(8,128)(2,1)} %slice.48.theirs_ref.refs_9_, bf16[512,3072]{1,0:T(8,128)(2,1)} %own_ref.3, ...), custom_call_target="tpu_custom_call" | custom-call | flops 1150000000 | tf_op jit(solution)/shard_map/front_query/pallas_call | solution.py:160
  41.4 1.8 collective-permute-start.2
  43.2 6.0 %all-to-all-start = ((bf16[16,64,256]{2,1,0:T(8,128)(2,1)}), bf16[16,64,256]{2,1,0:T(8,128)(2,1)}, u32[]{:S(2)}, u32[]{:S(2)}) async-start(bf16[16,64,256]{2,1,0:T(8,128)(2,1)} %get-tuple-element.85), calls=%async_computation | async-start | bytes 1048576 | tf_op jit(solution)/shard_map/all_to_all | solution.py:995
  49.2 17.7 %collective-permute-done.2.rest_1_.rest_4_.rn_ref = bf16[256,2048]{1,0:T(8,128)(2,1)S(1)} collective-permute-done((bf16[256,2048]{1,0:T(8,128)(2,1)}, bf16[256,2048]{1,0:T(8,128)(2,1)S(1)}, u32[]{:S(2)}, u32[]{:S(2)}) %collective-permute-start.2) | collective-permute-done | bytes 1048608 | tf_op jit(solution)/shard_map/ppermute | solution.py:978
  66.8 2.8 collective-permute-done.3.rest_2_.rest_5_.rf_ref
  69.6 6.1 %front_rest.1 = bf16[16,2,64,256]{3,2,1,0:T(8,128)(2,1)} custom-call(s32[5]{0:T(128)} %stack.38.place, bf16[256,1024]{1,0:T(8,128)(2,1)} %get-tuple-element.87.h_ref, bf16[16,1024]{1,0:T(8,128)(2,1)} %get-tuple-element.82.mine_ref.refs_8_, bf16[16,1024]{1,0:T(8,128)(2,1)} %slice.48.theirs_ref.refs_9_, bf16[512,3072]{1,0:T(8,128)(2,1)} %own_ref.3, ...), custom_call_target="tpu_custom_call" | custom-call | flops 1150000000 | tf_op jit(solution)/shard_map/front_rest/pallas_call | solution.py:210
  75.7 6.4 %all-to-all-start.1 = ((bf16[16,2,64,256]{3,2,1,0:T(8,128)(2,1)}), bf16[16,2,64,256]{3,2,1,0:T(8,128)(2,1)}, u32[]{:S(2)}, u32[]{:S(2)}) async-start(bf16[16,2,64,256]{3,2,1,0:T(8,128)(2,1)} %front_rest.1), calls=%async_computation.1 | async-start | bytes 2097152 | tf_op jit(solution)/shard_map/all_to_all | solution.py:995
  82.1 2.8 constant_dynamic-slice_fusion.5
  87.8 23.1 %collective-permute-done.9.refs_11_.en0_ref = bf16[256,2048]{1,0:T(8,128)(2,1)S(1)} collective-permute-done((bf16[256,2048]{1,0:T(8,128)(2,1)S(1)}, bf16[256,2048]{1,0:T(8,128)(2,1)S(1)}, u32[]{:S(2)}, u32[]{:S(2)}) %collective-permute-start.9) | collective-permute-done | bytes 1048608 | tf_op jit(solution)/shard_map/ppermute | solution.py:978
  112.4 14.5 %attend.1 = (bf16[16,64,256]{2,1,0:T(8,128)(2,1)}, f32[16,64,256]{2,1,0:T(8,128)}, f32[4,8,512]{2,1,0:T(8,128)}) custom-call(bf16[16,64,256]{2,1,0:T(8,128)(2,1)} %all-to-all-done.query_ref, bf16[16,2,64,256]{3,2,1,0:T(8,128)(2,1)} %all-to-all-done.1.kv_ref), custom_call_target="tpu_custom_call" | custom-call | flops 1150000000 | tf_op jit(solution)/shard_map/attend/pallas_call | solution.py:303
  127.0 6.9 %all-to-all-start.2 = ((bf16[16,64,256]{2,1,0:T(8,128)(2,1)}), bf16[16,64,256]{2,1,0:T(8,128)(2,1)}, u32[]{:S(2)}, u32[]{:S(2)}) async-start(bf16[16,64,256]{2,1,0:T(8,128)(2,1)} %get-tuple-element.90), calls=%async_computation.2 | async-start | bytes 1048576 | tf_op jit(solution)/shard_map/all_to_all | solution.py:995
  134.5 9.6 %collective-permute-done.10.refs_12_.en1_ref = bf16[256,2048]{1,0:T(8,128)(2,1)} collective-permute-done((bf16[256,2048]{1,0:T(8,128)(2,1)}, bf16[256,2048]{1,0:T(8,128)(2,1)}, u32[]{:S(2)}, u32[]{:S(2)}) %collective-permute-start.10) | collective-permute-done | bytes 1048608 | tf_op jit(solution)/shard_map/ppermute | solution.py:978
  145.6 11.0 %all-to-all-done.2 = bf16[16,64,256]{2,1,0:T(8,128)(2,1)} async-done(((bf16[16,64,256]{2,1,0:T(8,128)(2,1)}), bf16[16,64,256]{2,1,0:T(8,128)(2,1)}, u32[]{:S(2)}, u32[]{:S(2)}) %all-to-all-start.2) | async-done | bytes 524320 | tf_op jit(solution)/shard_map/all_to_all | solution.py:995
  156.5 4.8 %merge.1 = (f32[256,1024]{1,0:T(8,128)}, bf16[256,1024]{1,0:T(8,128)(2,1)}, bf16[256,1024]{1,0:T(8,128)(2,1)}) custom-call(s32[5]{0:T(128)} %stack.38.place, bf16[256,1024]{1,0:T(8,128)(2,1)} %bitcast.82, bf16[1024,256]{1,0:T(8,128)(2,1)} %bitcast.6.ot_ref, bf16[16,1024]{1,0:T(8,128)(2,1)} %get-tuple-element.82.mine_ref.refs_8_, ...), custom_call_target="tpu_custom_call" | custom-call | flops 1150000000 | tf_op jit(solution)/shard_map/merge/pallas_call | solution.py:438
  163.1 12.2 %collective-permute-done.6.refs_1_ = bf16[256,1024]{1,0:T(8,128)(2,1)S(1)} collective-permute-done((bf16[256,1024]{1,0:T(8,128)(2,1)}, bf16[256,1024]{1,0:T(8,128)(2,1)S(1)}, u32[]{:S(2)}, u32[]{:S(2)}) %collective-permute-start.6) | collective-permute-done | bytes 524320 | tf_op jit(solution)/shard_map/ppermute | solution.py:978
  178.0 23.8 %mlp_weights.1 = (bf16[1024,1024]{1,0:T(8,128)(2,1)}, bf16[8,128,1024]{2,1,0:T(8,128)(2,1)}) custom-call(s32[5]{0:T(128)} %stack.38.place, bf16[256,1024]{1,0:T(8,128)(2,1)} %get-tuple-element.94.refs_0_.h_ref, bf16[256,1024]{1,0:T(8,128)(2,1)} %copy-done.10, bf16[256,1024]{1,0:T(8,128)(2,1)} %copy-done.11, bf16[256,1024]{1,0:T(8,128)(2,1)} %copy-done.13, ...), custom_call_target="tpu_custom_call" | custom-call | flops 1150000000 | tf_op jit(solution)/shard_map/mlp_weights/pallas_call | solution.py:689
  203.2 2.9 collective-permute-start.16
  206.1 21.0 %mlp.1 = (bf16[256,1024]{1,0:T(8,128)(2,1)}, f32[256,1024]{1,0:T(8,128)}, bf16[272,1024]{1,0:T(8,128)(2,1)}, bf16[1024,256]{1,0:T(8,128)(2,1)}) custom-call(s32[5]{0:T(128)} %stack.38.place, f32[256,1024]{1,0:T(8,128)} %get-tuple-element.105.x1_ref, bf16[256,1024]{1,0:T(8,128)(2,1)} %get-tuple-element.94.refs_0_.h_ref, bf16[256,1024]{1,0:T(8,128)(2,1)} %bitcast.78, ...), custom_call_target="tpu_custom_call" | custom-call | flops 1150000000 | tf_op jit(solution)/shard_map/mlp/pallas_call | solution.py:588
  227.5 8.9 %all-to-all-start.3 = ((bf16[16,64,256]{2,1,0:T(8,128)(2,1)}), bf16[16,64,256]{2,1,0:T(8,128)(2,1)S(1)}, u32[]{:S(2)}, u32[]{:S(2)}) async-start(bf16[16,64,256]{2,1,0:T(8,128)(2,1)} %bitcast.89), calls=%async_computation.3 | async-start | bytes 1048576 | tf_op jit(solution)/shard_map/all_to_all | solution.py:995
  239.8 2.9 collective-permute-done.23.refs_5_
  243.2 2.0 fusion
  246.0 6.1 %collective-permute-start.17 = (bf16[128,1024]{1,0:T(8,128)(2,1)}, bf16[128,1024]{1,0:T(8,128)(2,1)}, u32[]{:S(2)}, u32[]{:S(2)}) collective-permute-start(bf16[128,1024]{1,0:T(8,128)(2,1)} %get-tuple-element.153), channel_id=1, source_target_pairs={{0,8},{2,10},{4,12},{6,14},{8,16},{10,18},{12,20},{14,22},{16,24},... | collective-permute-start | bytes 786440 | tf_op jit(solution)/shard_map/ppermute | solution.py:987
  252.1 1.9 collective-permute-start.18
  254.7 4.1 merge_weights.1
  258.8 2.2 collective-permute-done.17
  261.0 10.6 %collective-permute-done.18 = bf16[128,1024]{1,0:T(8,128)(2,1)} collective-permute-done((bf16[128,1024]{1,0:T(8,128)(2,1)}, bf16[128,1024]{1,0:T(8,128)(2,1)}, u32[]{:S(2)}, u32[]{:S(2)}) %collective-permute-start.18) | collective-permute-done | bytes 262176 | tf_op jit(solution)/shard_map/ppermute | solution.py:987
  273.0 11.3 %collective-permute-start.26 = (bf16[128,1024]{1,0:T(8,128)(2,1)S(1)}, bf16[128,1024]{1,0:T(8,128)(2,1)S(1)}, u32[]{:S(2)}, u32[]{:S(2)}) collective-permute-start(bf16[128,1024]{1,0:T(8,128)(2,1)S(1)} %fusion.4), channel_id=1, source_target_pairs={{0,8},{2,10},{4,12},{6,14},{8,16},{10,18},{12,20},{14,22},{16,24},... | collective-permute-start | bytes 786440 | tf_op jit(solution)/shard_map/ppermute | solution.py:987
  286.7 20.1 %attend_back.1.dp_ref = bf16[16,3,64,256]{3,2,1,0:T(8,128)(2,1)} custom-call(bf16[16,64,256]{2,1,0:T(8,128)(2,1)} %all-to-all-done.query_ref, bf16[16,2,64,256]{3,2,1,0:T(8,128)(2,1)} %all-to-all-done.1.kv_ref, bf16[16,64,256]{2,1,0:T(8,128)(2,1)} %copy-done.8, f32[16,64,256]{2,1,0:T(8,128)} %get-tuple-element.127.of_ref, ...), custom_call_target="tpu_custom_call" | custom-call | flops 1150000000 | tf_op jit(solution)/shard_map/attend_back/pallas_call | solution.py:397
  307.7 5.9 %all-to-all-start.4 = ((bf16[16,3,64,256]{3,2,1,0:T(8,128)(2,1)}), bf16[16,3,64,256]{3,2,1,0:T(8,128)(2,1)S(1)}, u32[]{:S(2)}, u32[]{:S(2)}) async-start(bf16[16,3,64,256]{3,2,1,0:T(8,128)(2,1)} %attend_back.1.dp_ref), calls=%async_computation.4 | async-start | bytes 3145728 | tf_op jit(solution)/shard_map/all_to_all | solution.py:995
  314.5 1.9 collective-permute-start.30
  316.4 12.6 %heads_gradient.1 = f32[192,1024]{1,0:T(8,128)} custom-call(bf16[16,3,64,256]{3,2,1,0:T(8,128)(2,1)} %attend_back.1.dp_ref, bf16[16,256,1024]{2,1,0:T(8,128)(2,1)} %bitcast.73), custom_call_target="tpu_custom_call" | custom-call | flops 1150000000 | tf_op jit(solution)/shard_map/heads_gradient/pallas_call | solution.py:830
  331.4 2.2 pad_maximum_fusion.refs_0_
  333.7 6.8 %collective-permute-done.30 = bf16[4,48,1024]{2,1,0:T(8,128)(2,1)} collective-permute-done((bf16[4,48,1024]{2,1,0:T(8,128)(2,1)}, bf16[4,48,1024]{2,1,0:T(8,128)(2,1)}, u32[]{:S(2)}, u32[]{:S(2)}) %collective-permute-start.30) | collective-permute-done | bytes 393248 | tf_op jit(solution)/shard_map/ppermute | solution.py:984
  341.8 3.6 collective-permute-start.32
  345.7 9.4 %collective-permute-done.31 = bf16[48,1024]{1,0:T(8,128)(2,1)S(1)} collective-permute-done((bf16[48,1024]{1,0:T(8,128)(2,1)S(1)}, bf16[48,1024]{1,0:T(8,128)(2,1)S(1)}, u32[]{:S(2)}, u32[]{:S(2)}) %collective-permute-start.31) | collective-permute-done | bytes 98336 | tf_op jit(solution)/shard_map/ppermute | solution.py:987
  355.1 21.4 %collective-permute-done.32 = bf16[48,1024]{1,0:T(8,128)(2,1)S(1)} collective-permute-done((bf16[48,1024]{1,0:T(8,128)(2,1)S(1)}, bf16[48,1024]{1,0:T(8,128)(2,1)S(1)}, u32[]{:S(2)}, u32[]{:S(2)}) %collective-permute-start.32) | collective-permute-done | bytes 98336 | tf_op jit(solution)/shard_map/ppermute | solution.py:987
  378.4 10.7 %all-gather.13.cloned.1.call-done = bf16[2048,1024]{1,0:T(8,128)(2,1)} async-done(((bf16[128,1024]{1,0:T(8,128)(2,1)}), bf16[2048,1024]{1,0:T(8,128)(2,1)}) %all-gather.13.cloned.1.call-update) | async-done | bytes 4194320 | tf_op jit(solution)/shard_map/all_gather | solution.py:1105
  389.8 8.2 %back.1 = (f32[256,1024]{1,0:T(8,128)}, f32[8,1024]{1,0:T(8,128)}) custom-call(s32[5]{0:T(128)} %stack.38.place, bf16[16,3,64,256]{3,2,1,0:T(8,128)(2,1)} %copy-done.1, bf16[256,1024]{1,0:T(8,128)(2,1)} %bitcast.83, f32[256,1024]{1,0:T(8,128)} %get-tuple-element.141.dx_ref, bf16[16,1024]{1,0:T(8,128)(2,1)} %get-tuple-element.82.mine_ref.refs_8_, ...), custom_call_target="tpu_custom_call" | custom-call | flops 1150000000 | tf_op jit(solution)/shard_map/back/pallas_call | solution.py:930
  400.0 2.5 collective-permute-done.35
  403.2 3.5 all-to-all-start.5
  406.7 7.3 %spread_expand.1 = f32[512,4096]{1,0:T(8,128)} custom-call(bf16[16,128,1024]{2,1,0:T(8,128)(2,1)} %bitcast.76), custom_call_target="tpu_custom_call" | custom-call | flops 1150000000 | tf_op jit(solution)/shard_map/spread_expand/pallas_call | solution.py:767
  415.9 12.2 %spread_contract.1 = f32[2048,1024]{1,0:T(8,128)} custom-call(s32[5]{0:T(128)} %stack.38.place, bf16[4,128,1024]{2,1,0:T(8,128)(2,1)} %pad_maximum_fusion.refs_0_, bf16[4,128,1024]{2,1,0:T(8,128)(2,1)} %collective-permute-done.34.refs_1_, bf16[4,128,1024]{2,1,0:T(8,128)(2,1)} %collective-permute-done.36.refs_2_, ...), custom_call_target="tpu_custom_call" | custom-call | flops 1150000000 | tf_op jit(solution)/shard_map/spread_contract/pallas_call | solution.py:803
  428.1 17.3 %all-gather.15.cloned.1.call-done = bf16[2304,1024]{1,0:T(8,128)(2,1)} async-done(((bf16[144,1024]{1,0:T(8,128)(2,1)}), bf16[2304,1024]{1,0:T(8,128)(2,1)}) %all-gather.15.cloned.1.call-update) | async-done | bytes 4718608 | tf_op jit(solution)/shard_map/all_gather | solution.py:1142
  445.4 6.8 %spread_heads.1 = (f32[512,3072]{1,0:T(8,128)}, f32[2,8,32,1024]{3,2,1,0:T(8,128)}) custom-call(bf16[16,144,1024]{2,1,0:T(8,128)(2,1)} %bitcast.74), custom_call_target="tpu_custom_call" | custom-call | flops 1150000000 | tf_op jit(solution)/shard_map/spread_heads/pallas_call | solution.py:875
  (144 shorter events, 40.9 us)
Async XLA Ops:
  7.2 170.0 %all-gather.9.cloned.1.call-start = ((), (), s32[]{:S(2)}) async-start(), calls=%async_computation.8 | async-start | bytes 4456448 | tf_op jit(solution)/shard_map/all_gather | solution.py:1024
  10.7 21.4 %collective-permute-start = (bf16[400,1024]{1,0:T(8,128)(2,1)}, bf16[400,1024]{1,0:T(8,128)(2,1)S(1)}, u32[]{:S(2)}, u32[]{:S(2)}) collective-permute-start(bf16[400,1024]{1,0:T(8,128)(2,1)} %get-tuple-element.83), channel_id=1, source_target_pairs={{0,1},{1,0},{2,3},{3,2},{4,5},{5,4},{6,7},{7,6},{8,9},{9,8},{10,11... | collective-permute-start | bytes 2457608 | tf_op jit(solution)/shard_map/ppermute | solution.py:978
  32.9 170.3 %all-gather.11.cloned.1.call-start = ((), (), s32[]{:S(2)}) async-start(), calls=%async_computation.9 | async-start | bytes 8912896 | tf_op jit(solution)/shard_map/all_gather | solution.py:1039
  33.0 2.0 collective-permute-start.1
  41.4 25.5 %collective-permute-start.2 = (bf16[256,2048]{1,0:T(8,128)(2,1)}, bf16[256,2048]{1,0:T(8,128)(2,1)S(1)}, u32[]{:S(2)}, u32[]{:S(2)}) collective-permute-start(bf16[256,2048]{1,0:T(8,128)(2,1)} %constant_dynamic-slice_fusion.8), channel_id=1, source_target_pairs={{0,1},{1,0},{2,3},{3,2},{4,5},{5,4},{6,7},{7,6},{8,9},{9,8},{10,11... | collective-permute-start | bytes 3145736 | tf_op jit(solution)/shard_map/ppermute | solution.py:978
  43.2 23.7 %all-to-all-start = ((bf16[16,64,256]{2,1,0:T(8,128)(2,1)}), bf16[16,64,256]{2,1,0:T(8,128)(2,1)}, u32[]{:S(2)}, u32[]{:S(2)}) async-start(bf16[16,64,256]{2,1,0:T(8,128)(2,1)} %get-tuple-element.85), calls=%async_computation | async-start | bytes 1048576 | tf_op jit(solution)/shard_map/all_to_all | solution.py:995
  66.8 2.8 collective-permute-start.3
  75.7 36.7 %all-to-all-start.1 = ((bf16[16,2,64,256]{3,2,1,0:T(8,128)(2,1)}), bf16[16,2,64,256]{3,2,1,0:T(8,128)(2,1)}, u32[]{:S(2)}, u32[]{:S(2)}) async-start(bf16[16,2,64,256]{3,2,1,0:T(8,128)(2,1)} %front_rest.1), calls=%async_computation.1 | async-start | bytes 2097152 | tf_op jit(solution)/shard_map/all_to_all | solution.py:995
  84.9 26.0 %collective-permute-start.9 = (bf16[256,2048]{1,0:T(8,128)(2,1)S(1)}, bf16[256,2048]{1,0:T(8,128)(2,1)S(1)}, u32[]{:S(2)}, u32[]{:S(2)}) collective-permute-start(bf16[256,2048]{1,0:T(8,128)(2,1)S(1)} %get-tuple-element.96), channel_id=1, source_target_pairs={{0,1},{1,0},{2,3},{3,2},{4,5},{5,4},{6,7},{7,6},{8,9},{9,8},{10,11... | collective-permute-start | bytes 3145736 | tf_op jit(solution)/shard_map/ppermute | solution.py:978
  87.3 46.6 %collective-permute-start.4 = (bf16[256,1024]{1,0:T(8,128)(2,1)}, bf16[256,1024]{1,0:T(8,128)(2,1)}, u32[]{:S(2)}, u32[]{:S(2)}) collective-permute-start(bf16[256,1024]{1,0:T(8,128)(2,1)} %constant_dynamic-slice_fusion.6), channel_id=1, source_target_pairs={{0,1},{1,0},{2,3},{3,2},{4,5},{5,4},{6,7},{7,6},{8,9},{9,8},{10,11... | collective-permute-start | bytes 1572872 | tf_op jit(solution)/shard_map/ppermute | solution.py:978
  110.9 33.1 %collective-permute-start.10 = (bf16[256,2048]{1,0:T(8,128)(2,1)}, bf16[256,2048]{1,0:T(8,128)(2,1)}, u32[]{:S(2)}, u32[]{:S(2)}) collective-permute-start(bf16[256,2048]{1,0:T(8,128)(2,1)} %get-tuple-element.97), channel_id=1, source_target_pairs={{0,1},{1,0},{2,3},{3,2},{4,5},{5,4},{6,7},{7,6},{8,9},{9,8},{10,11... | collective-permute-start | bytes 3145736 | tf_op jit(solution)/shard_map/ppermute | solution.py:978
  127.0 29.6 %all-to-all-start.2 = ((bf16[16,64,256]{2,1,0:T(8,128)(2,1)}), bf16[16,64,256]{2,1,0:T(8,128)(2,1)}, u32[]{:S(2)}, u32[]{:S(2)}) async-start(bf16[16,64,256]{2,1,0:T(8,128)(2,1)} %get-tuple-element.90), calls=%async_computation.2 | async-start | bytes 1048576 | tf_op jit(solution)/shard_map/all_to_all | solution.py:995
  133.8 173.0 %reduce-scatter.2.cloned.1.call-start = ((), (), s32[]{:S(2)}) async-start(), calls=%async_computation.7 | async-start | bytes 2359296 | tf_op jit(solution)/shard_map/reduce_scatter | solution.py:1066
  133.9 11.7 %collective-permute-start.5 = (bf16[256,1024]{1,0:T(8,128)(2,1)}, bf16[256,1024]{1,0:T(8,128)(2,1)}, u32[]{:S(2)}, u32[]{:S(2)}) collective-permute-start(bf16[256,1024]{1,0:T(8,128)(2,1)} %collective-permute-done.4.mn_ref), channel_id=1, source_target_pairs={{0,2},{2,0},{4,6},{6,4},{8,10},{10,8},{12,14},{14,12},{16,18},{18,... | collective-permute-start | bytes 1572872 | tf_op jit(solution)/shard_map/ppermute | solution.py:981
  134.3 28.7 %collective-permute-start.14 = (bf16[256,2048]{1,0:T(8,128)(2,1)S(1)}, bf16[256,2048]{1,0:T(8,128)(2,1)}, u32[]{:S(2)}, u32[]{:S(2)}) collective-permute-start(bf16[256,2048]{1,0:T(8,128)(2,1)S(1)} %collective-permute-done.9.refs_11_.en0_ref), channel_id=1, source_target_pairs={{0,2},{2,0},{4,6},{6,4},{8,10},{10,8},{12,14},{14,12},{16,18},{18,... | collective-permute-start | bytes 3145736 | tf_op jit(solution)/shard_map/ppermute | solution.py:981
  144.1 18.5 %collective-permute-start.11 = (bf16[256,1024]{1,0:T(8,128)(2,1)S(1)}, bf16[256,1024]{1,0:T(8,128)(2,1)}, u32[]{:S(2)}, u32[]{:S(2)}) collective-permute-start(bf16[256,1024]{1,0:T(8,128)(2,1)S(1)} %bitcast.79), channel_id=1, source_target_pairs={{0,1},{1,0},{2,3},{3,2},{4,5},{5,4},{6,7},{7,6},{8,9},{9,8},{10,11... | collective-permute-start | bytes 1572872 | tf_op jit(solution)/shard_map/ppermute | solution.py:978
  145.6 29.7 %collective-permute-start.15 = (bf16[256,2048]{1,0:T(8,128)(2,1)}, bf16[256,2048]{1,0:T(8,128)(2,1)}, u32[]{:S(2)}, u32[]{:S(2)}) collective-permute-start(bf16[256,2048]{1,0:T(8,128)(2,1)} %collective-permute-done.10.refs_12_.en1_ref), channel_id=1, source_target_pairs={{0,2},{2,0},{4,6},{6,4},{8,10},{10,8},{12,14},{14,12},{16,18},{18,... | collective-permute-start | bytes 3145736 | tf_op jit(solution)/shard_map/ppermute | solution.py:981
  161.4 13.9 %collective-permute-start.6 = (bf16[256,1024]{1,0:T(8,128)(2,1)}, bf16[256,1024]{1,0:T(8,128)(2,1)S(1)}, u32[]{:S(2)}, u32[]{:S(2)}) collective-permute-start(bf16[256,1024]{1,0:T(8,128)(2,1)} %get-tuple-element.94.refs_0_.h_ref), channel_id=1, source_target_pairs={{0,1},{1,0},{2,3},{3,2},{4,5},{5,4},{6,7},{7,6},{8,9},{9,8},{10,11... | collective-permute-start | bytes 1572872 | tf_op jit(solution)/shard_map/ppermute | solution.py:978
  162.5 12.8 %collective-permute-start.7 = (bf16[256,1024]{1,0:T(8,128)(2,1)}, bf16[256,1024]{1,0:T(8,128)(2,1)S(1)}, u32[]{:S(2)}, u32[]{:S(2)}) collective-permute-start(bf16[256,1024]{1,0:T(8,128)(2,1)} %get-tuple-element.94.refs_0_.h_ref), channel_id=1, source_target_pairs={{0,2},{2,0},{4,6},{6,4},{8,10},{10,8},{12,14},{14,12},{16,18},{18,... | collective-permute-start | bytes 1572872 | tf_op jit(solution)/shard_map/ppermute | solution.py:981
  162.5 12.8 %collective-permute-start.12 = (bf16[256,1024]{1,0:T(8,128)(2,1)S(1)}, bf16[256,1024]{1,0:T(8,128)(2,1)}, u32[]{:S(2)}, u32[]{:S(2)}) collective-permute-start(bf16[256,1024]{1,0:T(8,128)(2,1)S(1)} %bitcast.80), channel_id=1, source_target_pairs={{0,2},{2,0},{4,6},{6,4},{8,10},{10,8},{12,14},{14,12},{16,18},{18,... | collective-permute-start | bytes 1572872 | tf_op jit(solution)/shard_map/ppermute | solution.py:981
  163.0 13.1 %collective-permute-start.13 = (bf16[256,1024]{1,0:T(8,128)(2,1)}, bf16[256,1024]{1,0:T(8,128)(2,1)S(1)}, u32[]{:S(2)}, u32[]{:S(2)}) collective-permute-start(bf16[256,1024]{1,0:T(8,128)(2,1)} %collective-permute-done.11.refs_5_), channel_id=1, source_target_pairs={{0,2},{2,0},{4,6},{6,4},{8,10},{10,8},{12,14},{14,12},{16,18},{18,... | collective-permute-start | bytes 1572872 | tf_op jit(solution)/shard_map/ppermute | solution.py:981
  203.2 39.4 %collective-permute-start.16 = (bf16[4,128,1024]{2,1,0:T(8,128)(2,1)S(1)}, bf16[4,128,1024]{2,1,0:T(8,128)(2,1)}, u32[]{:S(2)}, u32[]{:S(2)}) collective-permute-start(bf16[4,128,1024]{2,1,0:T(8,128)(2,1)S(1)} %dynamic-slice_bitcast_fusion), channel_id=1, source_target_pairs={{0,4},{2,6},{4,0},{6,2},{8,12},{10,14},{12,8},{14,10},{16,20},{18,... | collective-permute-start | bytes 3145736 | tf_op jit(solution)/shard_map/ppermute | solution.py:984
  227.1 15.5 %collective-permute-start.23 = (bf16[272,1024]{1,0:T(8,128)(2,1)}, bf16[272,1024]{1,0:T(8,128)(2,1)S(1)}, u32[]{:S(2)}, u32[]{:S(2)}) collective-permute-start(bf16[272,1024]{1,0:T(8,128)(2,1)} %get-tuple-element.115.refs_4_), channel_id=1, source_target_pairs={{0,1},{1,0},{2,3},{3,2},{4,5},{5,4},{6,7},{7,6},{8,9},{9,8},{10,11... | collective-permute-start | bytes 1671176 | tf_op jit(solution)/shard_map/ppermute | solution.py:978
  227.5 45.5 %all-to-all-start.3 = ((bf16[16,64,256]{2,1,0:T(8,128)(2,1)}), bf16[16,64,256]{2,1,0:T(8,128)(2,1)S(1)}, u32[]{:S(2)}, u32[]{:S(2)}) async-start(bf16[16,64,256]{2,1,0:T(8,128)(2,1)} %bitcast.89), calls=%async_computation.3 | async-start | bytes 1048576 | tf_op jit(solution)/shard_map/all_to_all | solution.py:995
  236.4 152.7 %all-gather.13.cloned.1.call-start = ((), (), s32[]{:S(2)}) async-start(), calls=%async_computation.10 | async-start | bytes 4456448 | tf_op jit(solution)/shard_map/all_gather | solution.py:1105
  237.6 8.4 %collective-permute-start.20 = (bf16[256,256]{1,0:T(8,128)(2,1)S(1)}, bf16[256,256]{1,0:T(8,128)(2,1)S(1)}, u32[]{:S(2)}, u32[]{:S(2)}) collective-permute-start(bf16[256,256]{1,0:T(8,128)(2,1)S(1)} %get-tuple-element.156), channel_id=1, source_target_pairs={{0,1},{1,0},{2,3},{3,2},{4,5},{5,4},{6,7},{7,6},{8,9},{9,8},{10,11... | collective-permute-start | bytes 393224 | tf_op jit(solution)/shard_map/ppermute | solution.py:978
  239.0 13.1 %collective-permute-start.21 = (bf16[256,256]{1,0:T(8,128)(2,1)S(1)}, bf16[256,256]{1,0:T(8,128)(2,1)S(1)}, u32[]{:S(2)}, u32[]{:S(2)}) collective-permute-start(bf16[256,256]{1,0:T(8,128)(2,1)S(1)} %get-tuple-element.155), channel_id=1, source_target_pairs={{0,2},{2,0},{4,6},{6,4},{8,10},{10,8},{12,14},{14,12},{16,18},{18,... | collective-permute-start | bytes 393224 | tf_op jit(solution)/shard_map/ppermute | solution.py:981
  239.1 14.9 %collective-permute-start.22 = (bf16[256,256]{1,0:T(8,128)(2,1)S(1)}, bf16[256,256]{1,0:T(8,128)(2,1)S(1)}, u32[]{:S(2)}, u32[]{:S(2)}) collective-permute-start(bf16[256,256]{1,0:T(8,128)(2,1)S(1)} %get-tuple-element.154), channel_id=1, source_target_pairs={{0,3},{1,2},{2,1},{3,0},{4,7},{5,6},{6,5},{7,4},{8,11},{9,10},{10,... | collective-permute-start | bytes 393224 | tf_op jit(solution)/shard_map/ppermute | solution.py:992
  242.6 12.1 %collective-permute-start.24 = (bf16[272,1024]{1,0:T(8,128)(2,1)}, bf16[272,1024]{1,0:T(8,128)(2,1)}, u32[]{:S(2)}, u32[]{:S(2)}) collective-permute-start(bf16[272,1024]{1,0:T(8,128)(2,1)} %get-tuple-element.115.refs_4_), channel_id=1, source_target_pairs={{0,2},{2,0},{4,6},{6,4},{8,10},{10,8},{12,14},{14,12},{16,18},{18,... | collective-permute-start | bytes 1671176 | tf_op jit(solution)/shard_map/ppermute | solution.py:981
  242.7 12.1 %collective-permute-start.25 = (bf16[272,1024]{1,0:T(8,128)(2,1)S(1)}, bf16[272,1024]{1,0:T(8,128)(2,1)}, u32[]{:S(2)}, u32[]{:S(2)}) collective-permute-start(bf16[272,1024]{1,0:T(8,128)(2,1)S(1)} %collective-permute-done.23.refs_5_), channel_id=1, source_target_pairs={{0,2},{2,0},{4,6},{6,4},{8,10},{10,8},{12,14},{14,12},{16,18},{18,... | collective-permute-start | bytes 1671176 | tf_op jit(solution)/shard_map/ppermute | solution.py:981
  246.0 15.0 %collective-permute-start.17 = (bf16[128,1024]{1,0:T(8,128)(2,1)}, bf16[128,1024]{1,0:T(8,128)(2,1)}, u32[]{:S(2)}, u32[]{:S(2)}) collective-permute-start(bf16[128,1024]{1,0:T(8,128)(2,1)} %get-tuple-element.153), channel_id=1, source_target_pairs={{0,8},{2,10},{4,12},{6,14},{8,16},{10,18},{12,20},{14,22},{16,24},... | collective-permute-start | bytes 786440 | tf_op jit(solution)/shard_map/ppermute | solution.py:987
  252.1 19.6 %collective-permute-start.18 = (bf16[128,1024]{1,0:T(8,128)(2,1)}, bf16[128,1024]{1,0:T(8,128)(2,1)}, u32[]{:S(2)}, u32[]{:S(2)}) collective-permute-start(bf16[128,1024]{1,0:T(8,128)(2,1)} %get-tuple-element.152), channel_id=1, source_target_pairs={{0,16},{2,18},{4,20},{6,22},{8,24},{10,26},{12,28},{14,30},{16,0},... | collective-permute-start | bytes 786440 | tf_op jit(solution)/shard_map/ppermute | solution.py:987
  254.0 17.6 %collective-permute-start.19 = (bf16[128,1024]{1,0:T(8,128)(2,1)S(1)}, bf16[128,1024]{1,0:T(8,128)(2,1)}, u32[]{:S(2)}, u32[]{:S(2)}) collective-permute-start(bf16[128,1024]{1,0:T(8,128)(2,1)S(1)} %get-tuple-element.151), channel_id=1, source_target_pairs={{0,24},{2,26},{4,28},{6,30},{8,0},{10,2},{12,4},{14,6},{16,8},{18,... | collective-permute-start | bytes 786440 | tf_op jit(solution)/shard_map/ppermute | solution.py:987
  273.0 33.8 %collective-permute-start.26 = (bf16[128,1024]{1,0:T(8,128)(2,1)S(1)}, bf16[128,1024]{1,0:T(8,128)(2,1)S(1)}, u32[]{:S(2)}, u32[]{:S(2)}) collective-permute-start(bf16[128,1024]{1,0:T(8,128)(2,1)S(1)} %fusion.4), channel_id=1, source_target_pairs={{0,8},{2,10},{4,12},{6,14},{8,16},{10,18},{12,20},{14,22},{16,24},... | collective-permute-start | bytes 786440 | tf_op jit(solution)/shard_map/ppermute | solution.py:987
  284.3 22.6 %collective-permute-start.27 = (bf16[128,1024]{1,0:T(8,128)(2,1)S(1)}, bf16[128,1024]{1,0:T(8,128)(2,1)S(1)}, u32[]{:S(2)}, u32[]{:S(2)}) collective-permute-start(bf16[128,1024]{1,0:T(8,128)(2,1)S(1)} %fusion.4), channel_id=1, source_target_pairs={{0,16},{2,18},{4,20},{6,22},{8,24},{10,26},{12,28},{14,30},{16,0},... | collective-permute-start | bytes 786440 | tf_op jit(solution)/shard_map/ppermute | solution.py:987
  285.3 21.6 %collective-permute-start.28 = (bf16[128,1024]{1,0:T(8,128)(2,1)S(1)}, bf16[128,1024]{1,0:T(8,128)(2,1)S(1)}, u32[]{:S(2)}, u32[]{:S(2)}) collective-permute-start(bf16[128,1024]{1,0:T(8,128)(2,1)S(1)} %fusion.4), channel_id=1, source_target_pairs={{0,24},{2,26},{4,28},{6,30},{8,0},{10,2},{12,4},{14,6},{16,8},{18,... | collective-permute-start | bytes 786440 | tf_op jit(solution)/shard_map/ppermute | solution.py:987
  307.7 70.7 %all-to-all-start.4 = ((bf16[16,3,64,256]{3,2,1,0:T(8,128)(2,1)}), bf16[16,3,64,256]{3,2,1,0:T(8,128)(2,1)S(1)}, u32[]{:S(2)}, u32[]{:S(2)}) async-start(bf16[16,3,64,256]{3,2,1,0:T(8,128)(2,1)} %attend_back.1.dp_ref), calls=%async_computation.4 | async-start | bytes 3145728 | tf_op jit(solution)/shard_map/all_to_all | solution.py:995
  313.6 131.8 %all-gather.15.cloned.1.call-start = ((), (), s32[]{:S(2)}) async-start(), calls=%async_computation.11 | async-start | bytes 5013504 | tf_op jit(solution)/shard_map/all_gather | solution.py:1142
  314.5 26.0 %collective-permute-start.30 = (bf16[4,48,1024]{2,1,0:T(8,128)(2,1)}, bf16[4,48,1024]{2,1,0:T(8,128)(2,1)}, u32[]{:S(2)}, u32[]{:S(2)}) collective-permute-start(bf16[4,48,1024]{2,1,0:T(8,128)(2,1)} %dynamic-slice_bitcast_fusion.1), channel_id=1, source_target_pairs={{0,4},{2,6},{4,0},{6,2},{8,12},{10,14},{12,8},{14,10},{16,20},{18,... | collective-permute-start | bytes 1179656 | tf_op jit(solution)/shard_map/ppermute | solution.py:984
  330.1 15.6 %collective-permute-start.29 = (bf16[192,512]{1,0:T(8,128)(2,1)S(1)}, bf16[192,512]{1,0:T(8,128)(2,1)S(1)}, u32[]{:S(2)}, u32[]{:S(2)}) collective-permute-start(bf16[192,512]{1,0:T(8,128)(2,1)S(1)} %dynamic-slice_convert_fusion), channel_id=1, source_target_pairs={{0,1},{1,0},{2,3},{3,2},{4,5},{5,4},{6,7},{7,6},{8,9},{9,8},{10,11... | collective-permute-start | bytes 589832 | tf_op jit(solution)/shard_map/ppermute | solution.py:978
  333.6 44.8 %collective-permute-start.34 = (bf16[4,128,1024]{2,1,0:T(8,128)(2,1)}, bf16[4,128,1024]{2,1,0:T(8,128)(2,1)}, u32[]{:S(2)}, u32[]{:S(2)}) collective-permute-start(bf16[4,128,1024]{2,1,0:T(8,128)(2,1)} %pad_maximum_fusion.refs_0_), channel_id=1, source_target_pairs={{0,4},{2,6},{4,0},{6,2},{8,12},{10,14},{12,8},{14,10},{16,20},{18,... | collective-permute-start | bytes 3145736 | tf_op jit(solution)/shard_map/ppermute | solution.py:984
  341.8 13.3 %collective-permute-start.31 = (bf16[48,1024]{1,0:T(8,128)(2,1)S(1)}, bf16[48,1024]{1,0:T(8,128)(2,1)S(1)}, u32[]{:S(2)}, u32[]{:S(2)}) collective-permute-start(bf16[48,1024]{1,0:T(8,128)(2,1)S(1)} %get-tuple-element.159), channel_id=1, source_target_pairs={{0,8},{2,10},{4,12},{6,14},{8,16},{10,18},{12,20},{14,22},{16,24},... | collective-permute-start | bytes 294920 | tf_op jit(solution)/shard_map/ppermute | solution.py:987
  341.8 34.6 %collective-permute-start.32 = (bf16[48,1024]{1,0:T(8,128)(2,1)S(1)}, bf16[48,1024]{1,0:T(8,128)(2,1)S(1)}, u32[]{:S(2)}, u32[]{:S(2)}) collective-permute-start(bf16[48,1024]{1,0:T(8,128)(2,1)S(1)} %get-tuple-element.158), channel_id=1, source_target_pairs={{0,16},{2,18},{4,20},{6,22},{8,24},{10,26},{12,28},{14,30},{16,0},... | collective-permute-start | bytes 294920 | tf_op jit(solution)/shard_map/ppermute | solution.py:987
  345.4 31.0 %collective-permute-start.33 = (bf16[48,1024]{1,0:T(8,128)(2,1)S(1)}, bf16[48,1024]{1,0:T(8,128)(2,1)S(1)}, u32[]{:S(2)}, u32[]{:S(2)}) collective-permute-start(bf16[48,1024]{1,0:T(8,128)(2,1)S(1)} %get-tuple-element.157), channel_id=1, source_target_pairs={{0,24},{2,26},{4,28},{6,30},{8,0},{10,2},{12,4},{14,6},{16,8},{18,... | collective-permute-start | bytes 294920 | tf_op jit(solution)/shard_map/ppermute | solution.py:987
  389.2 26.7 %collective-permute-start.36 = (bf16[4,128,1024]{2,1,0:T(8,128)(2,1)}, bf16[4,128,1024]{2,1,0:T(8,128)(2,1)}, u32[]{:S(2)}, u32[]{:S(2)}) collective-permute-start(bf16[4,128,1024]{2,1,0:T(8,128)(2,1)} %pad_maximum_fusion.refs_0_), channel_id=1, source_target_pairs={{0,2},{2,0},{4,6},{6,4},{8,10},{10,8},{12,14},{14,12},{16,18},{18,... | collective-permute-start | bytes 3145736 | tf_op jit(solution)/shard_map/ppermute | solution.py:981
  389.5 26.4 %collective-permute-start.37 = (bf16[4,128,1024]{2,1,0:T(8,128)(2,1)}, bf16[4,128,1024]{2,1,0:T(8,128)(2,1)}, u32[]{:S(2)}, u32[]{:S(2)}) collective-permute-start(bf16[4,128,1024]{2,1,0:T(8,128)(2,1)} %collective-permute-done.34.refs_1_), channel_id=1, source_target_pairs={{0,2},{2,0},{4,6},{6,4},{8,10},{10,8},{12,14},{14,12},{16,18},{18,... | collective-permute-start | bytes 3145736 | tf_op jit(solution)/shard_map/ppermute | solution.py:981
  398.8 3.7 collective-permute-start.35
  403.2 12.0 %all-to-all-start.5 = ((f32[16,4,512]{2,1,0:T(4,128)}), f32[16,4,512]{2,1,0:T(4,128)S(1)}, u32[]{:S(2)}, u32[]{:S(2)}) async-start(f32[16,4,512]{2,1,0:T(4,128)} %broadcast_in_dim.3), calls=%async_computation.6 | async-start | bytes 262144 | tf_op jit(solution)/shard_map/all_to_all | solution.py:995
  (22 other events, 207.2 us)
Sparse Core Ops, SparseCore 0:
  33.0 68.1 all-gather.8
  103.4 81.0 all-gather.10
  203.4 83.9 reduce-scatter.1
  307.0 82.0 all-gather.12
  391.3 54.0 all-gather.14
where the time goes:
time: 469 us; the launch traced here: 461 us
  waiting for transfers between devices  181 us (39%)
  Pallas kernels  150 us (32%)
  starting transfers between devices  87.2 us (19%)
  local copies, waits for them, and re-layouts  19.9 us (4%)
  between operations  14.6 us (3%)
  other arithmetic  8.38 us (2%)
    ppermute x11, waiting for transfers between devices, over_x(): return lax.ppermute(value, 'fsdp', [(0, 1), (1, 0)])  84.1 us
    ppermute x9, waiting for transfers between devices, on_ring(): lax.ppermute(value, 'ctx', [(i, (i + 4 * by) % nctx) for i in range(nctx)])  43.6 us
    all_to_all x6, starting transfers between devices, exchange(): return lax.all_to_all(value, 'ctx', 0, 0)  37.6 us
    ppermute x9, starting transfers between devices, on_ring(): lax.ppermute(value, 'ctx', [(i, (i + 4 * by) % nctx) for i in range(nctx)])  26.1 us
    pallas_call x1, Pallas kernels, mlp_weights(): pl.pallas_call(functools.partial(weights_body, own_steps), grid_spec=pltp...  23.8 us
    pallas_call x1, Pallas kernels, mlp(): pl.pallas_call(mlp_body, grid_spec=pltpu.PrefetchScalarGridSpec(num_scala...  21 us
    pallas_call x1, Pallas kernels, attend_back(): pl.pallas_call(functools.partial(attend_back_body, per, tokens, block, ch...  20.1 us
    all_gather x1, waiting for transfers between devices, per_device(): spread = lax.all_gather(spread, 'ctx', axis=0, tiled=False)  17.3 us
  transfers between devices with their start and end apart: 49, of which 20 were waited for; matrix products, arithmetic and copies ran while one was open for 5% of the time, Pallas kernels for 30%

commit v1 on v0

--- a/solution.py
+++ b/solution.py
@@ -843,40 +843,47 @@
 
 
 def spread_heads_body(begin, in_ref, heads_ref, merge_ref):
-    heads, _, width = in_ref.shape
+    some, _, width = in_ref.shape
     half = width // 2
     rows = 3 * HEAD // 2
+    now = pl.program_id(1)
+
+    def turn(part):
+        pieces = []
+        for head in range(some):
+            for row in range(part * HEAD, (part + 1) * HEAD, 32):
+                side = row // rows
+                here = row - side * rows
+                pieces.append(in_ref[head, here : here + 32, side * half : (side + 1) * half].astype(F32))
+        heads_ref[...] = jnp.concatenate(pieces, axis=0).T
+
+    for part in range(3):
+
+        @pl.when(now == part)
+        def _():
+            turn(part)
+
+    @pl.when(now == 0)
+    def _():
+        _, chips, rows, _ = merge_ref.shape
+        for chip in range(chips):
+            for core in range(2):
+                merge_ref[core, chip] = in_ref[2 * chip + core, begin : begin + rows, :].astype(F32)
+
+
+def spread_heads(gathered, begin, shape, merge_shape):
+    devices, rows, width = gathered.shape
     some = 4
-    for part in range(3):
-        for first in range(0, heads, some):
-            turned = []
-            for head in range(first, first + some):
-                for row in range(part * HEAD, (part + 1) * HEAD, 32):
-                    side = row // rows
-                    here = row - side * rows
-                    turned.append(in_ref[head, here : here + 32, side * half : (side + 1) * half])
-            piece = jnp.concatenate([member.astype(F32) for member in turned], axis=0)
-            column = (part * heads + first) * HEAD
-            heads_ref[:, column : column + some * HEAD] = piece.T
-    if merge_ref is not None:
-        spread_merge_body(begin, in_ref, merge_ref)
-
-
-def spread_merge_body(begin, in_ref, merge_ref):
-    _, chips, rows, _ = merge_ref.shape
-    for chip in range(chips):
-        for core in range(2):
-            merge_ref[core, chip] = in_ref[2 * chip + core, begin : begin + rows, :].astype(F32)
-
-
-def spread_heads(gathered, begin, shape, merge_shape):
-    devices, _, width = gathered.shape
+    steps = devices // some
     chunked = (2, devices // 2, merge_shape[0] // devices, width)
     heads, merged = pl.pallas_call(
         functools.partial(spread_heads_body, begin),
-        grid=(1,),
-        in_specs=[whole(gathered.shape)],
-        out_specs=[whole(shape), whole(chunked)],
+        grid=(steps, 3),
+        in_specs=[pl.BlockSpec((some, rows, width), lambda i, j: (i, 0, 0))],
+        out_specs=[
+            pl.BlockSpec((shape[0], some * HEAD), lambda i, j: (0, j * steps + i)),
+            pl.BlockSpec((2, some // 2) + chunked[2:], lambda i, j: (0, i, 0, 0)),
+        ],
         out_shape=[jax.ShapeDtypeStruct(shape, F32), jax.ShapeDtypeStruct(chunked, F32)],
         compiler_params=params(),
         cost_estimate=about(1),

time: 469 us -> 474 us (1.011)
  no operation moved by 1% of the time
where the time goes in v1:
time: 474 us; the launch traced here: 466 us
  waiting for transfers between devices  181 us (38%)
  Pallas kernels  154 us (32%)
  starting transfers between devices  87.2 us (18%)
  local copies, waits for them, and re-layouts  19.9 us (4%)
  between operations  14.6 us (3%)
  other arithmetic  8.38 us (2%)
    ppermute x11, waiting for transfers between devices, over_x(): return lax.ppermute(value, 'fsdp', [(0, 1), (1, 0)])  84.1 us
    ppermute x9, waiting for transfers between devices, on_ring(): lax.ppermute(value, 'ctx', [(i, (i + 4 * by) % nctx) for i in range(nctx)])  43.6 us
    all_to_all x6, starting transfers between devices, exchange(): return lax.all_to_all(value, 'ctx', 0, 0)  37.6 us
    ppermute x9, starting transfers between devices, on_ring(): lax.ppermute(value, 'ctx', [(i, (i + 4 * by) % nctx) for i in range(nctx)])  26.1 us
    pallas_call x1, Pallas kernels, mlp_weights(): pl.pallas_call(functools.partial(weights_body, own_steps), grid_spec=pltp...  23.8 us
    pallas_call x1, Pallas kernels, mlp(): pl.pallas_call(mlp_body, grid_spec=pltpu.PrefetchScalarGridSpec(num_scala...  21 us
    pallas_call x1, Pallas kernels, attend_back(): pl.pallas_call(functools.partial(attend_back_body, per, tokens, block, ch...  20.1 us
    all_gather x1, waiting for transfers between devices, per_device(): spread = lax.all_gather(spread, 'ctx', axis=0, tiled=False)  17.3 us
  transfers between devices with their start and end apart: 49, of which 20 were waited for; matrix products, arithmetic and copies ran while one was open for 5% of the time, Pallas kernels for 30%

profile of v1, /device:TPU:0, one launch (start us, length us, event | category | flops | bytes accessed | tf_op | source)
XLA Modules:
  0.0 465.6 jit_solution(8515454595001501934)
XLA Ops:
  7.9 2.9 parcel.1
  10.7 2.9 collective-permute-start
  13.7 2.3 constant_dynamic-slice_fusion.8
  16.0 16.1 %collective-permute-done = bf16[400,1024]{1,0:T(8,128)(2,1)S(1)} collective-permute-done((bf16[400,1024]{1,0:T(8,128)(2,1)}, bf16[400,1024]{1,0:T(8,128)(2,1)S(1)}, u32[]{:S(2)}, u32[]{:S(2)}) %collective-permute-start) | collective-permute-done | bytes 819232 | tf_op jit(solution)/shard_map/ppermute | solution.py:985
  35.8 5.6 %front_query.1 = (bf16[16,64,256]{2,1,0:T(8,128)(2,1)}, bf16[256,1024]{1,0:T(8,128)(2,1)}) custom-call(s32[5]{0:T(128)} %stack.38.place, bf16[256,1024]{1,0:T(8,128)(2,1)} %bitcast.81, bf16[16,1024]{1,0:T(8,128)(2,1)} %get-tuple-element.82.mine_ref.refs_8_, bf16[16,1024]{1,0:T(8,128)(2,1)} %slice.48.theirs_ref.refs_9_, bf16[512,3072]{1,0:T(8,128)(2,1)} %own_ref.3, ...), custom_call_target="tpu_custom_call" | custom-call | flops 1150000000 | tf_op jit(solution)/shard_map/front_query/pallas_call | solution.py:160
  41.4 1.8 collective-permute-start.2
  43.2 6.0 %all-to-all-start = ((bf16[16,64,256]{2,1,0:T(8,128)(2,1)}), bf16[16,64,256]{2,1,0:T(8,128)(2,1)}, u32[]{:S(2)}, u32[]{:S(2)}) async-start(bf16[16,64,256]{2,1,0:T(8,128)(2,1)} %get-tuple-element.85), calls=%async_computation | async-start | bytes 1048576 | tf_op jit(solution)/shard_map/all_to_all | solution.py:1002
  49.2 17.7 %collective-permute-done.2.rest_1_.rest_4_.rn_ref = bf16[256,2048]{1,0:T(8,128)(2,1)S(1)} collective-permute-done((bf16[256,2048]{1,0:T(8,128)(2,1)}, bf16[256,2048]{1,0:T(8,128)(2,1)S(1)}, u32[]{:S(2)}, u32[]{:S(2)}) %collective-permute-start.2) | collective-permute-done | bytes 1048608 | tf_op jit(solution)/shard_map/ppermute | solution.py:985
  66.8 2.8 collective-permute-done.3.rest_2_.rest_5_.rf_ref
  69.6 6.1 %front_rest.1 = bf16[16,2,64,256]{3,2,1,0:T(8,128)(2,1)} custom-call(s32[5]{0:T(128)} %stack.38.place, bf16[256,1024]{1,0:T(8,128)(2,1)} %get-tuple-element.87.h_ref, bf16[16,1024]{1,0:T(8,128)(2,1)} %get-tuple-element.82.mine_ref.refs_8_, bf16[16,1024]{1,0:T(8,128)(2,1)} %slice.48.theirs_ref.refs_9_, bf16[512,3072]{1,0:T(8,128)(2,1)} %own_ref.3, ...), custom_call_target="tpu_custom_call" | custom-call | flops 1150000000 | tf_op jit(solution)/shard_map/front_rest/pallas_call | solution.py:210
  75.7 6.4 %all-to-all-start.1 = ((bf16[16,2,64,256]{3,2,1,0:T(8,128)(2,1)}), bf16[16,2,64,256]{3,2,1,0:T(8,128)(2,1)}, u32[]{:S(2)}, u32[]{:S(2)}) async-start(bf16[16,2,64,256]{3,2,1,0:T(8,128)(2,1)} %front_rest.1), calls=%async_computation.1 | async-start | bytes 2097152 | tf_op jit(solution)/shard_map/all_to_all | solution.py:1002
  82.1 2.8 constant_dynamic-slice_fusion.5
  87.8 23.1 %collective-permute-done.9.refs_11_.en0_ref = bf16[256,2048]{1,0:T(8,128)(2,1)S(1)} collective-permute-done((bf16[256,2048]{1,0:T(8,128)(2,1)S(1)}, bf16[256,2048]{1,0:T(8,128)(2,1)S(1)}, u32[]{:S(2)}, u32[]{:S(2)}) %collective-permute-start.9) | collective-permute-done | bytes 1048608 | tf_op jit(solution)/shard_map/ppermute | solution.py:985
  112.4 14.5 %attend.1 = (bf16[16,64,256]{2,1,0:T(8,128)(2,1)}, f32[16,64,256]{2,1,0:T(8,128)}, f32[4,8,512]{2,1,0:T(8,128)}) custom-call(bf16[16,64,256]{2,1,0:T(8,128)(2,1)} %all-to-all-done.query_ref, bf16[16,2,64,256]{3,2,1,0:T(8,128)(2,1)} %all-to-all-done.1.kv_ref), custom_call_target="tpu_custom_call" | custom-call | flops 1150000000 | tf_op jit(solution)/shard_map/attend/pallas_call | solution.py:303
  127.0 6.9 %all-to-all-start.2 = ((bf16[16,64,256]{2,1,0:T(8,128)(2,1)}), bf16[16,64,256]{2,1,0:T(8,128)(2,1)}, u32[]{:S(2)}, u32[]{:S(2)}) async-start(bf16[16,64,256]{2,1,0:T(8,128)(2,1)} %get-tuple-element.90), calls=%async_computation.2 | async-start | bytes 1048576 | tf_op jit(solution)/shard_map/all_to_all | solution.py:1002
  134.5 9.6 %collective-permute-done.10.refs_12_.en1_ref = bf16[256,2048]{1,0:T(8,128)(2,1)} collective-permute-done((bf16[256,2048]{1,0:T(8,128)(2,1)}, bf16[256,2048]{1,0:T(8,128)(2,1)}, u32[]{:S(2)}, u32[]{:S(2)}) %collective-permute-start.10) | collective-permute-done | bytes 1048608 | tf_op jit(solution)/shard_map/ppermute | solution.py:985
  145.6 11.0 %all-to-all-done.2 = bf16[16,64,256]{2,1,0:T(8,128)(2,1)} async-done(((bf16[16,64,256]{2,1,0:T(8,128)(2,1)}), bf16[16,64,256]{2,1,0:T(8,128)(2,1)}, u32[]{:S(2)}, u32[]{:S(2)}) %all-to-all-start.2) | async-done | bytes 524320 | tf_op jit(solution)/shard_map/all_to_all | solution.py:1002
  156.5 4.8 %merge.1 = (f32[256,1024]{1,0:T(8,128)}, bf16[256,1024]{1,0:T(8,128)(2,1)}, bf16[256,1024]{1,0:T(8,128)(2,1)}) custom-call(s32[5]{0:T(128)} %stack.38.place, bf16[256,1024]{1,0:T(8,128)(2,1)} %bitcast.82, bf16[1024,256]{1,0:T(8,128)(2,1)} %bitcast.6.ot_ref, bf16[16,1024]{1,0:T(8,128)(2,1)} %get-tuple-element.82.mine_ref.refs_8_, ...), custom_call_target="tpu_custom_call" | custom-call | flops 1150000000 | tf_op jit(solution)/shard_map/merge/pallas_call | solution.py:438
  163.1 12.2 %collective-permute-done.6.refs_1_ = bf16[256,1024]{1,0:T(8,128)(2,1)S(1)} collective-permute-done((bf16[256,1024]{1,0:T(8,128)(2,1)}, bf16[256,1024]{1,0:T(8,128)(2,1)S(1)}, u32[]{:S(2)}, u32[]{:S(2)}) %collective-permute-start.6) | collective-permute-done | bytes 524320 | tf_op jit(solution)/shard_map/ppermute | solution.py:985
  178.0 23.8 %mlp_weights.1 = (bf16[1024,1024]{1,0:T(8,128)(2,1)}, bf16[8,128,1024]{2,1,0:T(8,128)(2,1)}) custom-call(s32[5]{0:T(128)} %stack.38.place, bf16[256,1024]{1,0:T(8,128)(2,1)} %get-tuple-element.94.refs_0_.h_ref, bf16[256,1024]{1,0:T(8,128)(2,1)} %copy-done.10, bf16[256,1024]{1,0:T(8,128)(2,1)} %copy-done.11, bf16[256,1024]{1,0:T(8,128)(2,1)} %copy-done.13, ...), custom_call_target="tpu_custom_call" | custom-call | flops 1150000000 | tf_op jit(solution)/shard_map/mlp_weights/pallas_call | solution.py:689
  203.2 2.9 collective-permute-start.16
  206.1 21.0 %mlp.1 = (bf16[256,1024]{1,0:T(8,128)(2,1)}, f32[256,1024]{1,0:T(8,128)}, bf16[272,1024]{1,0:T(8,128)(2,1)}, bf16[1024,256]{1,0:T(8,128)(2,1)}) custom-call(s32[5]{0:T(128)} %stack.38.place, f32[256,1024]{1,0:T(8,128)} %get-tuple-element.105.x1_ref, bf16[256,1024]{1,0:T(8,128)(2,1)} %get-tuple-element.94.refs_0_.h_ref, bf16[256,1024]{1,0:T(8,128)(2,1)} %bitcast.78, ...), custom_call_target="tpu_custom_call" | custom-call | flops 1150000000 | tf_op jit(solution)/shard_map/mlp/pallas_call | solution.py:588
  227.5 8.9 %all-to-all-start.3 = ((bf16[16,64,256]{2,1,0:T(8,128)(2,1)}), bf16[16,64,256]{2,1,0:T(8,128)(2,1)S(1)}, u32[]{:S(2)}, u32[]{:S(2)}) async-start(bf16[16,64,256]{2,1,0:T(8,128)(2,1)} %bitcast.89), calls=%async_computation.3 | async-start | bytes 1048576 | tf_op jit(solution)/shard_map/all_to_all | solution.py:1002
  239.8 2.9 collective-permute-done.23.refs_5_
  243.2 2.0 fusion
  246.0 6.1 %collective-permute-start.17 = (bf16[128,1024]{1,0:T(8,128)(2,1)}, bf16[128,1024]{1,0:T(8,128)(2,1)}, u32[]{:S(2)}, u32[]{:S(2)}) collective-permute-start(bf16[128,1024]{1,0:T(8,128)(2,1)} %get-tuple-element.153), channel_id=1, source_target_pairs={{0,8},{2,10},{4,12},{6,14},{8,16},{10,18},{12,20},{14,22},{16,24},... | collective-permute-start | bytes 786440 | tf_op jit(solution)/shard_map/ppermute | solution.py:994
  252.1 1.9 collective-permute-start.18
  254.7 4.1 merge_weights.1
  258.8 2.2 collective-permute-done.17
  261.0 10.6 %collective-permute-done.18 = bf16[128,1024]{1,0:T(8,128)(2,1)} collective-permute-done((bf16[128,1024]{1,0:T(8,128)(2,1)}, bf16[128,1024]{1,0:T(8,128)(2,1)}, u32[]{:S(2)}, u32[]{:S(2)}) %collective-permute-start.18) | collective-permute-done | bytes 262176 | tf_op jit(solution)/shard_map/ppermute | solution.py:994
  273.0 11.3 %collective-permute-start.26 = (bf16[128,1024]{1,0:T(8,128)(2,1)S(1)}, bf16[128,1024]{1,0:T(8,128)(2,1)S(1)}, u32[]{:S(2)}, u32[]{:S(2)}) collective-permute-start(bf16[128,1024]{1,0:T(8,128)(2,1)S(1)} %fusion.4), channel_id=1, source_target_pairs={{0,8},{2,10},{4,12},{6,14},{8,16},{10,18},{12,20},{14,22},{16,24},... | collective-permute-start | bytes 786440 | tf_op jit(solution)/shard_map/ppermute | solution.py:994
  286.7 20.1 %attend_back.1.dp_ref = bf16[16,3,64,256]{3,2,1,0:T(8,128)(2,1)} custom-call(bf16[16,64,256]{2,1,0:T(8,128)(2,1)} %all-to-all-done.query_ref, bf16[16,2,64,256]{3,2,1,0:T(8,128)(2,1)} %all-to-all-done.1.kv_ref, bf16[16,64,256]{2,1,0:T(8,128)(2,1)} %copy-done.8, f32[16,64,256]{2,1,0:T(8,128)} %get-tuple-element.127.of_ref, ...), custom_call_target="tpu_custom_call" | custom-call | flops 1150000000 | tf_op jit(solution)/shard_map/attend_back/pallas_call | solution.py:397
  307.7 5.9 %all-to-all-start.4 = ((bf16[16,3,64,256]{3,2,1,0:T(8,128)(2,1)}), bf16[16,3,64,256]{3,2,1,0:T(8,128)(2,1)S(1)}, u32[]{:S(2)}, u32[]{:S(2)}) async-start(bf16[16,3,64,256]{3,2,1,0:T(8,128)(2,1)} %attend_back.1.dp_ref), calls=%async_computation.4 | async-start | bytes 3145728 | tf_op jit(solution)/shard_map/all_to_all | solution.py:1002
  314.5 1.9 collective-permute-start.30
  316.4 12.6 %heads_gradient.1 = f32[192,1024]{1,0:T(8,128)} custom-call(bf16[16,3,64,256]{3,2,1,0:T(8,128)(2,1)} %attend_back.1.dp_ref, bf16[16,256,1024]{2,1,0:T(8,128)(2,1)} %bitcast.73), custom_call_target="tpu_custom_call" | custom-call | flops 1150000000 | tf_op jit(solution)/shard_map/heads_gradient/pallas_call | solution.py:830
  331.4 2.2 pad_maximum_fusion.refs_0_
  333.7 6.8 %collective-permute-done.30 = bf16[4,48,1024]{2,1,0:T(8,128)(2,1)} collective-permute-done((bf16[4,48,1024]{2,1,0:T(8,128)(2,1)}, bf16[4,48,1024]{2,1,0:T(8,128)(2,1)}, u32[]{:S(2)}, u32[]{:S(2)}) %collective-permute-start.30) | collective-permute-done | bytes 393248 | tf_op jit(solution)/shard_map/ppermute | solution.py:991
  341.8 3.6 collective-permute-start.32
  345.7 9.4 %collective-permute-done.31 = bf16[48,1024]{1,0:T(8,128)(2,1)S(1)} collective-permute-done((bf16[48,1024]{1,0:T(8,128)(2,1)S(1)}, bf16[48,1024]{1,0:T(8,128)(2,1)S(1)}, u32[]{:S(2)}, u32[]{:S(2)}) %collective-permute-start.31) | collective-permute-done | bytes 98336 | tf_op jit(solution)/shard_map/ppermute | solution.py:994
  355.1 21.4 %collective-permute-done.32 = bf16[48,1024]{1,0:T(8,128)(2,1)S(1)} collective-permute-done((bf16[48,1024]{1,0:T(8,128)(2,1)S(1)}, bf16[48,1024]{1,0:T(8,128)(2,1)S(1)}, u32[]{:S(2)}, u32[]{:S(2)}) %collective-permute-start.32) | collective-permute-done | bytes 98336 | tf_op jit(solution)/shard_map/ppermute | solution.py:994
  378.4 10.7 %all-gather.13.cloned.1.call-done = bf16[2048,1024]{1,0:T(8,128)(2,1)} async-done(((bf16[128,1024]{1,0:T(8,128)(2,1)}), bf16[2048,1024]{1,0:T(8,128)(2,1)}) %all-gather.13.cloned.1.call-update) | async-done | bytes 4194320 | tf_op jit(solution)/shard_map/all_gather | solution.py:1112
  389.8 8.2 %back.1 = (f32[256,1024]{1,0:T(8,128)}, f32[8,1024]{1,0:T(8,128)}) custom-call(s32[5]{0:T(128)} %stack.38.place, bf16[16,3,64,256]{3,2,1,0:T(8,128)(2,1)} %copy-done.1, bf16[256,1024]{1,0:T(8,128)(2,1)} %bitcast.83, f32[256,1024]{1,0:T(8,128)} %get-tuple-element.141.dx_ref, bf16[16,1024]{1,0:T(8,128)(2,1)} %get-tuple-element.82.mine_ref.refs_8_, ...), custom_call_target="tpu_custom_call" | custom-call | flops 1150000000 | tf_op jit(solution)/shard_map/back/pallas_call | solution.py:937
  400.0 2.5 collective-permute-done.35
  403.2 3.5 all-to-all-start.5
  406.7 7.3 %spread_expand.1 = f32[512,4096]{1,0:T(8,128)} custom-call(bf16[16,128,1024]{2,1,0:T(8,128)(2,1)} %bitcast.76), custom_call_target="tpu_custom_call" | custom-call | flops 1150000000 | tf_op jit(solution)/shard_map/spread_expand/pallas_call | solution.py:767
  415.9 12.2 %spread_contract.1 = f32[2048,1024]{1,0:T(8,128)} custom-call(s32[5]{0:T(128)} %stack.38.place, bf16[4,128,1024]{2,1,0:T(8,128)(2,1)} %pad_maximum_fusion.refs_0_, bf16[4,128,1024]{2,1,0:T(8,128)(2,1)} %collective-permute-done.34.refs_1_, bf16[4,128,1024]{2,1,0:T(8,128)(2,1)} %collective-permute-done.36.refs_2_, ...), custom_call_target="tpu_custom_call" | custom-call | flops 1150000000 | tf_op jit(solution)/shard_map/spread_contract/pallas_call | solution.py:803
  428.1 17.3 %all-gather.15.cloned.1.call-done = bf16[2304,1024]{1,0:T(8,128)(2,1)} async-done(((bf16[144,1024]{1,0:T(8,128)(2,1)}), bf16[2304,1024]{1,0:T(8,128)(2,1)}) %all-gather.15.cloned.1.call-update) | async-done | bytes 4718608 | tf_op jit(solution)/shard_map/all_gather | solution.py:1149
  445.4 11.2 %spread_heads.1 = (f32[512,3072]{1,0:T(8,128)}, f32[2,8,32,1024]{3,2,1,0:T(8,128)}) custom-call(bf16[16,144,1024]{2,1,0:T(8,128)(2,1)} %bitcast.74), custom_call_target="tpu_custom_call" | custom-call | flops 1150000000 | tf_op jit(solution)/shard_map/spread_heads/pallas_call | solution.py:879
  (144 shorter events, 40.9 us)
Async XLA Ops:
  7.2 170.0 %all-gather.9.cloned.1.call-start = ((), (), s32[]{:S(2)}) async-start(), calls=%async_computation.8 | async-start | bytes 4456448 | tf_op jit(solution)/shard_map/all_gather | solution.py:1031
  10.7 21.4 %collective-permute-start = (bf16[400,1024]{1,0:T(8,128)(2,1)}, bf16[400,1024]{1,0:T(8,128)(2,1)S(1)}, u32[]{:S(2)}, u32[]{:S(2)}) collective-permute-start(bf16[400,1024]{1,0:T(8,128)(2,1)} %get-tuple-element.83), channel_id=1, source_target_pairs={{0,1},{1,0},{2,3},{3,2},{4,5},{5,4},{6,7},{7,6},{8,9},{9,8},{10,11... | collective-permute-start | bytes 2457608 | tf_op jit(solution)/shard_map/ppermute | solution.py:985
  32.9 170.3 %all-gather.11.cloned.1.call-start = ((), (), s32[]{:S(2)}) async-start(), calls=%async_computation.9 | async-start | bytes 8912896 | tf_op jit(solution)/shard_map/all_gather | solution.py:1046
  33.0 2.0 collective-permute-start.1
  41.4 25.5 %collective-permute-start.2 = (bf16[256,2048]{1,0:T(8,128)(2,1)}, bf16[256,2048]{1,0:T(8,128)(2,1)S(1)}, u32[]{:S(2)}, u32[]{:S(2)}) collective-permute-start(bf16[256,2048]{1,0:T(8,128)(2,1)} %constant_dynamic-slice_fusion.8), channel_id=1, source_target_pairs={{0,1},{1,0},{2,3},{3,2},{4,5},{5,4},{6,7},{7,6},{8,9},{9,8},{10,11... | collective-permute-start | bytes 3145736 | tf_op jit(solution)/shard_map/ppermute | solution.py:985
  43.2 23.7 %all-to-all-start = ((bf16[16,64,256]{2,1,0:T(8,128)(2,1)}), bf16[16,64,256]{2,1,0:T(8,128)(2,1)}, u32[]{:S(2)}, u32[]{:S(2)}) async-start(bf16[16,64,256]{2,1,0:T(8,128)(2,1)} %get-tuple-element.85), calls=%async_computation | async-start | bytes 1048576 | tf_op jit(solution)/shard_map/all_to_all | solution.py:1002
  66.8 2.8 collective-permute-start.3
  75.7 36.7 %all-to-all-start.1 = ((bf16[16,2,64,256]{3,2,1,0:T(8,128)(2,1)}), bf16[16,2,64,256]{3,2,1,0:T(8,128)(2,1)}, u32[]{:S(2)}, u32[]{:S(2)}) async-start(bf16[16,2,64,256]{3,2,1,0:T(8,128)(2,1)} %front_rest.1), calls=%async_computation.1 | async-start | bytes 2097152 | tf_op jit(solution)/shard_map/all_to_all | solution.py:1002
  84.9 26.0 %collective-permute-start.9 = (bf16[256,2048]{1,0:T(8,128)(2,1)S(1)}, bf16[256,2048]{1,0:T(8,128)(2,1)S(1)}, u32[]{:S(2)}, u32[]{:S(2)}) collective-permute-start(bf16[256,2048]{1,0:T(8,128)(2,1)S(1)} %get-tuple-element.96), channel_id=1, source_target_pairs={{0,1},{1,0},{2,3},{3,2},{4,5},{5,4},{6,7},{7,6},{8,9},{9,8},{10,11... | collective-permute-start | bytes 3145736 | tf_op jit(solution)/shard_map/ppermute | solution.py:985
  87.3 46.6 %collective-permute-start.4 = (bf16[256,1024]{1,0:T(8,128)(2,1)}, bf16[256,1024]{1,0:T(8,128)(2,1)}, u32[]{:S(2)}, u32[]{:S(2)}) collective-permute-start(bf16[256,1024]{1,0:T(8,128)(2,1)} %constant_dynamic-slice_fusion.6), channel_id=1, source_target_pairs={{0,1},{1,0},{2,3},{3,2},{4,5},{5,4},{6,7},{7,6},{8,9},{9,8},{10,11... | collective-permute-start | bytes 1572872 | tf_op jit(solution)/shard_map/ppermute | solution.py:985
  110.9 33.1 %collective-permute-start.10 = (bf16[256,2048]{1,0:T(8,128)(2,1)}, bf16[256,2048]{1,0:T(8,128)(2,1)}, u32[]{:S(2)}, u32[]{:S(2)}) collective-permute-start(bf16[256,2048]{1,0:T(8,128)(2,1)} %get-tuple-element.97), channel_id=1, source_target_pairs={{0,1},{1,0},{2,3},{3,2},{4,5},{5,4},{6,7},{7,6},{8,9},{9,8},{10,11... | collective-permute-start | bytes 3145736 | tf_op jit(solution)/shard_map/ppermute | solution.py:985
  127.0 29.6 %all-to-all-start.2 = ((bf16[16,64,256]{2,1,0:T(8,128)(2,1)}), bf16[16,64,256]{2,1,0:T(8,128)(2,1)}, u32[]{:S(2)}, u32[]{:S(2)}) async-start(bf16[16,64,256]{2,1,0:T(8,128)(2,1)} %get-tuple-element.90), calls=%async_computation.2 | async-start | bytes 1048576 | tf_op jit(solution)/shard_map/all_to_all | solution.py:1002
  133.8 173.0 %reduce-scatter.2.cloned.1.call-start = ((), (), s32[]{:S(2)}) async-start(), calls=%async_computation.7 | async-start | bytes 2359296 | tf_op jit(solution)/shard_map/reduce_scatter | solution.py:1073
  133.9 11.7 %collective-permute-start.5 = (bf16[256,1024]{1,0:T(8,128)(2,1)}, bf16[256,1024]{1,0:T(8,128)(2,1)}, u32[]{:S(2)}, u32[]{:S(2)}) collective-permute-start(bf16[256,1024]{1,0:T(8,128)(2,1)} %collective-permute-done.4.mn_ref), channel_id=1, source_target_pairs={{0,2},{2,0},{4,6},{6,4},{8,10},{10,8},{12,14},{14,12},{16,18},{18,... | collective-permute-start | bytes 1572872 | tf_op jit(solution)/shard_map/ppermute | solution.py:988
  134.3 28.7 %collective-permute-start.14 = (bf16[256,2048]{1,0:T(8,128)(2,1)S(1)}, bf16[256,2048]{1,0:T(8,128)(2,1)}, u32[]{:S(2)}, u32[]{:S(2)}) collective-permute-start(bf16[256,2048]{1,0:T(8,128)(2,1)S(1)} %collective-permute-done.9.refs_11_.en0_ref), channel_id=1, source_target_pairs={{0,2},{2,0},{4,6},{6,4},{8,10},{10,8},{12,14},{14,12},{16,18},{18,... | collective-permute-start | bytes 3145736 | tf_op jit(solution)/shard_map/ppermute | solution.py:988
  144.1 18.5 %collective-permute-start.11 = (bf16[256,1024]{1,0:T(8,128)(2,1)S(1)}, bf16[256,1024]{1,0:T(8,128)(2,1)}, u32[]{:S(2)}, u32[]{:S(2)}) collective-permute-start(bf16[256,1024]{1,0:T(8,128)(2,1)S(1)} %bitcast.79), channel_id=1, source_target_pairs={{0,1},{1,0},{2,3},{3,2},{4,5},{5,4},{6,7},{7,6},{8,9},{9,8},{10,11... | collective-permute-start | bytes 1572872 | tf_op jit(solution)/shard_map/ppermute | solution.py:985
  145.6 29.7 %collective-permute-start.15 = (bf16[256,2048]{1,0:T(8,128)(2,1)}, bf16[256,2048]{1,0:T(8,128)(2,1)}, u32[]{:S(2)}, u32[]{:S(2)}) collective-permute-start(bf16[256,2048]{1,0:T(8,128)(2,1)} %collective-permute-done.10.refs_12_.en1_ref), channel_id=1, source_target_pairs={{0,2},{2,0},{4,6},{6,4},{8,10},{10,8},{12,14},{14,12},{16,18},{18,... | collective-permute-start | bytes 3145736 | tf_op jit(solution)/shard_map/ppermute | solution.py:988
  161.4 13.9 %collective-permute-start.6 = (bf16[256,1024]{1,0:T(8,128)(2,1)}, bf16[256,1024]{1,0:T(8,128)(2,1)S(1)}, u32[]{:S(2)}, u32[]{:S(2)}) collective-permute-start(bf16[256,1024]{1,0:T(8,128)(2,1)} %get-tuple-element.94.refs_0_.h_ref), channel_id=1, source_target_pairs={{0,1},{1,0},{2,3},{3,2},{4,5},{5,4},{6,7},{7,6},{8,9},{9,8},{10,11... | collective-permute-start | bytes 1572872 | tf_op jit(solution)/shard_map/ppermute | solution.py:985
  162.5 12.8 %collective-permute-start.7 = (bf16[256,1024]{1,0:T(8,128)(2,1)}, bf16[256,1024]{1,0:T(8,128)(2,1)S(1)}, u32[]{:S(2)}, u32[]{:S(2)}) collective-permute-start(bf16[256,1024]{1,0:T(8,128)(2,1)} %get-tuple-element.94.refs_0_.h_ref), channel_id=1, source_target_pairs={{0,2},{2,0},{4,6},{6,4},{8,10},{10,8},{12,14},{14,12},{16,18},{18,... | collective-permute-start | bytes 1572872 | tf_op jit(solution)/shard_map/ppermute | solution.py:988
  162.5 12.8 %collective-permute-start.12 = (bf16[256,1024]{1,0:T(8,128)(2,1)S(1)}, bf16[256,1024]{1,0:T(8,128)(2,1)}, u32[]{:S(2)}, u32[]{:S(2)}) collective-permute-start(bf16[256,1024]{1,0:T(8,128)(2,1)S(1)} %bitcast.80), channel_id=1, source_target_pairs={{0,2},{2,0},{4,6},{6,4},{8,10},{10,8},{12,14},{14,12},{16,18},{18,... | collective-permute-start | bytes 1572872 | tf_op jit(solution)/shard_map/ppermute | solution.py:988
  163.0 13.1 %collective-permute-start.13 = (bf16[256,1024]{1,0:T(8,128)(2,1)}, bf16[256,1024]{1,0:T(8,128)(2,1)S(1)}, u32[]{:S(2)}, u32[]{:S(2)}) collective-permute-start(bf16[256,1024]{1,0:T(8,128)(2,1)} %collective-permute-done.11.refs_5_), channel_id=1, source_target_pairs={{0,2},{2,0},{4,6},{6,4},{8,10},{10,8},{12,14},{14,12},{16,18},{18,... | collective-permute-start | bytes 1572872 | tf_op jit(solution)/shard_map/ppermute | solution.py:988
  203.2 39.4 %collective-permute-start.16 = (bf16[4,128,1024]{2,1,0:T(8,128)(2,1)S(1)}, bf16[4,128,1024]{2,1,0:T(8,128)(2,1)}, u32[]{:S(2)}, u32[]{:S(2)}) collective-permute-start(bf16[4,128,1024]{2,1,0:T(8,128)(2,1)S(1)} %dynamic-slice_bitcast_fusion), channel_id=1, source_target_pairs={{0,4},{2,6},{4,0},{6,2},{8,12},{10,14},{12,8},{14,10},{16,20},{18,... | collective-permute-start | bytes 3145736 | tf_op jit(solution)/shard_map/ppermute | solution.py:991
  227.1 15.5 %collective-permute-start.23 = (bf16[272,1024]{1,0:T(8,128)(2,1)}, bf16[272,1024]{1,0:T(8,128)(2,1)S(1)}, u32[]{:S(2)}, u32[]{:S(2)}) collective-permute-start(bf16[272,1024]{1,0:T(8,128)(2,1)} %get-tuple-element.115.refs_4_), channel_id=1, source_target_pairs={{0,1},{1,0},{2,3},{3,2},{4,5},{5,4},{6,7},{7,6},{8,9},{9,8},{10,11... | collective-permute-start | bytes 1671176 | tf_op jit(solution)/shard_map/ppermute | solution.py:985
  227.5 45.5 %all-to-all-start.3 = ((bf16[16,64,256]{2,1,0:T(8,128)(2,1)}), bf16[16,64,256]{2,1,0:T(8,128)(2,1)S(1)}, u32[]{:S(2)}, u32[]{:S(2)}) async-start(bf16[16,64,256]{2,1,0:T(8,128)(2,1)} %bitcast.89), calls=%async_computation.3 | async-start | bytes 1048576 | tf_op jit(solution)/shard_map/all_to_all | solution.py:1002
  236.4 152.7 %all-gather.13.cloned.1.call-start = ((), (), s32[]{:S(2)}) async-start(), calls=%async_computation.10 | async-start | bytes 4456448 | tf_op jit(solution)/shard_map/all_gather | solution.py:1112
  237.6 8.4 %collective-permute-start.20 = (bf16[256,256]{1,0:T(8,128)(2,1)S(1)}, bf16[256,256]{1,0:T(8,128)(2,1)S(1)}, u32[]{:S(2)}, u32[]{:S(2)}) collective-permute-start(bf16[256,256]{1,0:T(8,128)(2,1)S(1)} %get-tuple-element.156), channel_id=1, source_target_pairs={{0,1},{1,0},{2,3},{3,2},{4,5},{5,4},{6,7},{7,6},{8,9},{9,8},{10,11... | collective-permute-start | bytes 393224 | tf_op jit(solution)/shard_map/ppermute | solution.py:985
  239.0 13.1 %collective-permute-start.21 = (bf16[256,256]{1,0:T(8,128)(2,1)S(1)}, bf16[256,256]{1,0:T(8,128)(2,1)S(1)}, u32[]{:S(2)}, u32[]{:S(2)}) collective-permute-start(bf16[256,256]{1,0:T(8,128)(2,1)S(1)} %get-tuple-element.155), channel_id=1, source_target_pairs={{0,2},{2,0},{4,6},{6,4},{8,10},{10,8},{12,14},{14,12},{16,18},{18,... | collective-permute-start | bytes 393224 | tf_op jit(solution)/shard_map/ppermute | solution.py:988
  239.1 14.9 %collective-permute-start.22 = (bf16[256,256]{1,0:T(8,128)(2,1)S(1)}, bf16[256,256]{1,0:T(8,128)(2,1)S(1)}, u32[]{:S(2)}, u32[]{:S(2)}) collective-permute-start(bf16[256,256]{1,0:T(8,128)(2,1)S(1)} %get-tuple-element.154), channel_id=1, source_target_pairs={{0,3},{1,2},{2,1},{3,0},{4,7},{5,6},{6,5},{7,4},{8,11},{9,10},{10,... | collective-permute-start | bytes 393224 | tf_op jit(solution)/shard_map/ppermute | solution.py:999
  242.6 12.1 %collective-permute-start.24 = (bf16[272,1024]{1,0:T(8,128)(2,1)}, bf16[272,1024]{1,0:T(8,128)(2,1)}, u32[]{:S(2)}, u32[]{:S(2)}) collective-permute-start(bf16[272,1024]{1,0:T(8,128)(2,1)} %get-tuple-element.115.refs_4_), channel_id=1, source_target_pairs={{0,2},{2,0},{4,6},{6,4},{8,10},{10,8},{12,14},{14,12},{16,18},{18,... | collective-permute-start | bytes 1671176 | tf_op jit(solution)/shard_map/ppermute | solution.py:988
  242.7 12.1 %collective-permute-start.25 = (bf16[272,1024]{1,0:T(8,128)(2,1)S(1)}, bf16[272,1024]{1,0:T(8,128)(2,1)}, u32[]{:S(2)}, u32[]{:S(2)}) collective-permute-start(bf16[272,1024]{1,0:T(8,128)(2,1)S(1)} %collective-permute-done.23.refs_5_), channel_id=1, source_target_pairs={{0,2},{2,0},{4,6},{6,4},{8,10},{10,8},{12,14},{14,12},{16,18},{18,... | collective-permute-start | bytes 1671176 | tf_op jit(solution)/shard_map/ppermute | solution.py:988
  246.0 15.0 %collective-permute-start.17 = (bf16[128,1024]{1,0:T(8,128)(2,1)}, bf16[128,1024]{1,0:T(8,128)(2,1)}, u32[]{:S(2)}, u32[]{:S(2)}) collective-permute-start(bf16[128,1024]{1,0:T(8,128)(2,1)} %get-tuple-element.153), channel_id=1, source_target_pairs={{0,8},{2,10},{4,12},{6,14},{8,16},{10,18},{12,20},{14,22},{16,24},... | collective-permute-start | bytes 786440 | tf_op jit(solution)/shard_map/ppermute | solution.py:994
  252.1 19.6 %collective-permute-start.18 = (bf16[128,1024]{1,0:T(8,128)(2,1)}, bf16[128,1024]{1,0:T(8,128)(2,1)}, u32[]{:S(2)}, u32[]{:S(2)}) collective-permute-start(bf16[128,1024]{1,0:T(8,128)(2,1)} %get-tuple-element.152), channel_id=1, source_target_pairs={{0,16},{2,18},{4,20},{6,22},{8,24},{10,26},{12,28},{14,30},{16,0},... | collective-permute-start | bytes 786440 | tf_op jit(solution)/shard_map/ppermute | solution.py:994
  254.0 17.6 %collective-permute-start.19 = (bf16[128,1024]{1,0:T(8,128)(2,1)S(1)}, bf16[128,1024]{1,0:T(8,128)(2,1)}, u32[]{:S(2)}, u32[]{:S(2)}) collective-permute-start(bf16[128,1024]{1,0:T(8,128)(2,1)S(1)} %get-tuple-element.151), channel_id=1, source_target_pairs={{0,24},{2,26},{4,28},{6,30},{8,0},{10,2},{12,4},{14,6},{16,8},{18,... | collective-permute-start | bytes 786440 | tf_op jit(solution)/shard_map/ppermute | solution.py:994
  273.0 33.8 %collective-permute-start.26 = (bf16[128,1024]{1,0:T(8,128)(2,1)S(1)}, bf16[128,1024]{1,0:T(8,128)(2,1)S(1)}, u32[]{:S(2)}, u32[]{:S(2)}) collective-permute-start(bf16[128,1024]{1,0:T(8,128)(2,1)S(1)} %fusion.4), channel_id=1, source_target_pairs={{0,8},{2,10},{4,12},{6,14},{8,16},{10,18},{12,20},{14,22},{16,24},... | collective-permute-start | bytes 786440 | tf_op jit(solution)/shard_map/ppermute | solution.py:994
  284.3 22.6 %collective-permute-start.27 = (bf16[128,1024]{1,0:T(8,128)(2,1)S(1)}, bf16[128,1024]{1,0:T(8,128)(2,1)S(1)}, u32[]{:S(2)}, u32[]{:S(2)}) collective-permute-start(bf16[128,1024]{1,0:T(8,128)(2,1)S(1)} %fusion.4), channel_id=1, source_target_pairs={{0,16},{2,18},{4,20},{6,22},{8,24},{10,26},{12,28},{14,30},{16,0},... | collective-permute-start | bytes 786440 | tf_op jit(solution)/shard_map/ppermute | solution.py:994
  285.3 21.6 %collective-permute-start.28 = (bf16[128,1024]{1,0:T(8,128)(2,1)S(1)}, bf16[128,1024]{1,0:T(8,128)(2,1)S(1)}, u32[]{:S(2)}, u32[]{:S(2)}) collective-permute-start(bf16[128,1024]{1,0:T(8,128)(2,1)S(1)} %fusion.4), channel_id=1, source_target_pairs={{0,24},{2,26},{4,28},{6,30},{8,0},{10,2},{12,4},{14,6},{16,8},{18,... | collective-permute-start | bytes 786440 | tf_op jit(solution)/shard_map/ppermute | solution.py:994
  307.7 70.7 %all-to-all-start.4 = ((bf16[16,3,64,256]{3,2,1,0:T(8,128)(2,1)}), bf16[16,3,64,256]{3,2,1,0:T(8,128)(2,1)S(1)}, u32[]{:S(2)}, u32[]{:S(2)}) async-start(bf16[16,3,64,256]{3,2,1,0:T(8,128)(2,1)} %attend_back.1.dp_ref), calls=%async_computation.4 | async-start | bytes 3145728 | tf_op jit(solution)/shard_map/all_to_all | solution.py:1002
  313.6 131.8 %all-gather.15.cloned.1.call-start = ((), (), s32[]{:S(2)}) async-start(), calls=%async_computation.11 | async-start | bytes 5013504 | tf_op jit(solution)/shard_map/all_gather | solution.py:1149
  314.5 26.0 %collective-permute-start.30 = (bf16[4,48,1024]{2,1,0:T(8,128)(2,1)}, bf16[4,48,1024]{2,1,0:T(8,128)(2,1)}, u32[]{:S(2)}, u32[]{:S(2)}) collective-permute-start(bf16[4,48,1024]{2,1,0:T(8,128)(2,1)} %dynamic-slice_bitcast_fusion.1), channel_id=1, source_target_pairs={{0,4},{2,6},{4,0},{6,2},{8,12},{10,14},{12,8},{14,10},{16,20},{18,... | collective-permute-start | bytes 1179656 | tf_op jit(solution)/shard_map/ppermute | solution.py:991
  330.1 15.6 %collective-permute-start.29 = (bf16[192,512]{1,0:T(8,128)(2,1)S(1)}, bf16[192,512]{1,0:T(8,128)(2,1)S(1)}, u32[]{:S(2)}, u32[]{:S(2)}) collective-permute-start(bf16[192,512]{1,0:T(8,128)(2,1)S(1)} %dynamic-slice_convert_fusion), channel_id=1, source_target_pairs={{0,1},{1,0},{2,3},{3,2},{4,5},{5,4},{6,7},{7,6},{8,9},{9,8},{10,11... | collective-permute-start | bytes 589832 | tf_op jit(solution)/shard_map/ppermute | solution.py:985
  333.6 44.8 %collective-permute-start.34 = (bf16[4,128,1024]{2,1,0:T(8,128)(2,1)}, bf16[4,128,1024]{2,1,0:T(8,128)(2,1)}, u32[]{:S(2)}, u32[]{:S(2)}) collective-permute-start(bf16[4,128,1024]{2,1,0:T(8,128)(2,1)} %pad_maximum_fusion.refs_0_), channel_id=1, source_target_pairs={{0,4},{2,6},{4,0},{6,2},{8,12},{10,14},{12,8},{14,10},{16,20},{18,... | collective-permute-start | bytes 3145736 | tf_op jit(solution)/shard_map/ppermute | solution.py:991
  341.8 13.3 %collective-permute-start.31 = (bf16[48,1024]{1,0:T(8,128)(2,1)S(1)}, bf16[48,1024]{1,0:T(8,128)(2,1)S(1)}, u32[]{:S(2)}, u32[]{:S(2)}) collective-permute-start(bf16[48,1024]{1,0:T(8,128)(2,1)S(1)} %get-tuple-element.159), channel_id=1, source_target_pairs={{0,8},{2,10},{4,12},{6,14},{8,16},{10,18},{12,20},{14,22},{16,24},... | collective-permute-start | bytes 294920 | tf_op jit(solution)/shard_map/ppermute | solution.py:994
  341.8 34.6 %collective-permute-start.32 = (bf16[48,1024]{1,0:T(8,128)(2,1)S(1)}, bf16[48,1024]{1,0:T(8,128)(2,1)S(1)}, u32[]{:S(2)}, u32[]{:S(2)}) collective-permute-start(bf16[48,1024]{1,0:T(8,128)(2,1)S(1)} %get-tuple-element.158), channel_id=1, source_target_pairs={{0,16},{2,18},{4,20},{6,22},{8,24},{10,26},{12,28},{14,30},{16,0},... | collective-permute-start | bytes 294920 | tf_op jit(solution)/shard_map/ppermute | solution.py:994
  345.4 31.0 %collective-permute-start.33 = (bf16[48,1024]{1,0:T(8,128)(2,1)S(1)}, bf16[48,1024]{1,0:T(8,128)(2,1)S(1)}, u32[]{:S(2)}, u32[]{:S(2)}) collective-permute-start(bf16[48,1024]{1,0:T(8,128)(2,1)S(1)} %get-tuple-element.157), channel_id=1, source_target_pairs={{0,24},{2,26},{4,28},{6,30},{8,0},{10,2},{12,4},{14,6},{16,8},{18,... | collective-permute-start | bytes 294920 | tf_op jit(solution)/shard_map/ppermute | solution.py:994
  389.2 26.7 %collective-permute-start.36 = (bf16[4,128,1024]{2,1,0:T(8,128)(2,1)}, bf16[4,128,1024]{2,1,0:T(8,128)(2,1)}, u32[]{:S(2)}, u32[]{:S(2)}) collective-permute-start(bf16[4,128,1024]{2,1,0:T(8,128)(2,1)} %pad_maximum_fusion.refs_0_), channel_id=1, source_target_pairs={{0,2},{2,0},{4,6},{6,4},{8,10},{10,8},{12,14},{14,12},{16,18},{18,... | collective-permute-start | bytes 3145736 | tf_op jit(solution)/shard_map/ppermute | solution.py:988
  389.5 26.4 %collective-permute-start.37 = (bf16[4,128,1024]{2,1,0:T(8,128)(2,1)}, bf16[4,128,1024]{2,1,0:T(8,128)(2,1)}, u32[]{:S(2)}, u32[]{:S(2)}) collective-permute-start(bf16[4,128,1024]{2,1,0:T(8,128)(2,1)} %collective-permute-done.34.refs_1_), channel_id=1, source_target_pairs={{0,2},{2,0},{4,6},{6,4},{8,10},{10,8},{12,14},{14,12},{16,18},{18,... | collective-permute-start | bytes 3145736 | tf_op jit(solution)/shard_map/ppermute | solution.py:988
  398.8 3.7 collective-permute-start.35
  403.2 12.0 %all-to-all-start.5 = ((f32[16,4,512]{2,1,0:T(4,128)}), f32[16,4,512]{2,1,0:T(4,128)S(1)}, u32[]{:S(2)}, u32[]{:S(2)}) async-start(f32[16,4,512]{2,1,0:T(4,128)} %broadcast_in_dim.3), calls=%async_computation.6 | async-start | bytes 262144 | tf_op jit(solution)/shard_map/all_to_all | solution.py:1002
  (22 other events, 207.2 us)
Sparse Core Ops, SparseCore 0:
  33.0 68.1 all-gather.8
  103.4 81.0 all-gather.10
  203.4 83.9 reduce-scatter.1
  307.0 82.0 all-gather.12
  391.3 54.0 all-gather.14
